TPU v7x, 32 devices: a whole 2x2x4 slice. The times are simulated.
32 devices in a mesh: dp: 4 (over y, x), row: 4 (over z), col: 2 (over core).
Axes of the slice: x: 2, y: 2, z: 4, core: 2. Of those that a mesh axis runs over, the one named last changes fastest.
Arguments:
- hidden_in: bfloat16 [32, 1024, 768], P(('dp', 'row'), None, 'col'), may hold values from -6 to 6
- encoded: bfloat16 [32, 256, 768], P(('dp', 'row'), None, 'col'), may hold values from -6 to 6
- cotangent: bfloat16 [32, 1024, 768], P(('dp', 'row'), None, 'col'), may hold values from -6 to 6
- piece_start: int32 [32, 2], P(('dp', 'row')), may hold values from 0 to 960, as said below
- image_piece_lengths: int32 [32, 2], P(('dp', 'row')), may hold values from 64 to 256, as said below
- bucket_table: int32 [2047], replicated, may hold values from 0 to 31
- self_query: bfloat16 [768, 768], P('row', 'col'), may hold values from -0.0546875 to 0.0546875
- self_key: bfloat16 [768, 768], P('row', 'col'), may hold values from -0.21875 to 0.21875
- self_value: bfloat16 [768, 768], P('row', 'col'), may hold values from -0.21875 to 0.21875
- self_out: bfloat16 [768, 768], P('col', 'row'), may hold values from -0.875 to 0.875
- rel_weight: bfloat16 [32, 12], P('row', 'col'), may hold values from -3 to 3
- cross_query: bfloat16 [768, 768], P('row', 'col'), may hold values from -0.0546875 to 0.0546875
- cross_key: bfloat16 [768, 768], P('row', 'col'), may hold values from -0.21875 to 0.21875
- cross_value: bfloat16 [768, 768], P('row', 'col'), may hold values from -0.21875 to 0.21875
- cross_out: bfloat16 [768, 768], P('col', 'row'), may hold values from -0.875 to 0.875
- ffn_gate: bfloat16 [768, 2048], P('row', 'col'), may hold values from -0.21875 to 0.21875
- ffn_up: bfloat16 [768, 2048], P('row', 'col'), may hold values from -0.21875 to 0.21875
- ffn_down: bfloat16 [2048, 768], P('col', 'row'), may hold values from -0.25 to 0.25
- gain_self: float32 [768], P('col'), may hold values from 0.25 to 1.75
- gain_cross: float32 [768], P('col'), may hold values from 0.25 to 1.75
- gain_ffn: float32 [768], P('col'), may hold values from 0.25 to 1.75
- gain_final: float32 [768], P('col'), may hold values from 0.25 to 1.75
Outputs:
- output: bfloat16 [32, 1024, 768], P(('dp', 'row'), None, 'col')
- hidden_grad: float32 [32, 1024, 768], P(('dp', 'row'), None, 'col')
- encoded_grad: float32 [32, 256, 768], P(('dp', 'row'), None, 'col')
- self_query_grad: float32 [768, 768], P('row', 'col')
- self_key_grad: float32 [768, 768], P('row', 'col')
- self_value_grad: float32 [768, 768], P('row', 'col')
- self_out_grad: float32 [768, 768], P('col', 'row')
- rel_weight_grad: float32 [32, 12], P('row', 'col')
- cross_query_grad: float32 [768, 768], P('row', 'col')
- cross_key_grad: float32 [768, 768], P('row', 'col')
- cross_value_grad: float32 [768, 768], P('row', 'col')
- cross_out_grad: float32 [768, 768], P('col', 'row')
- ffn_gate_grad: float32 [768, 2048], P('row', 'col')
- ffn_up_grad: float32 [768, 2048], P('row', 'col')
- ffn_down_grad: float32 [2048, 768], P('col', 'row')
- gain_self_grad: float32 [768], P('col')
- gain_cross_grad: float32 [768], P('col')
- gain_ffn_grad: float32 [768], P('col')
- gain_final_grad: float32 [768], P('col')
Inputs may be any that keep to these rules, and one draw needn't show every extreme that they name: `piece_start`: the p-th piece of a sequence lies inside positions p * 512 to (p + 1) * 512 - 1, so pieces never intersect. `image_piece_lengths`: some piece has exactly 256 tokens. `bucket_table`: entry j - i + 1023 is the bucket of a key at position j seen from a query at position i.
All inputs are finite; a program needn't handle non-finite values.
Results may differ from a plain program's by a relative error of at most 0.03.
The roundings to bfloat16 on the way count: a program that leaves them out, or rounds other values in their place, can miss the bound.
Values may be sent and summed in bfloat16 or wider, within the bound.
A program may use at most 256 MiB of HBM per device.

v0:
```python
import math

import jax
import jax.numpy as jnp
from jax import lax
from jax.sharding import PartitionSpec as P

D = 768
HEAD = 64
BUCKETS = 32
MB = 2


EPSILON = 1e-06
PRECISE = lax.Precision.HIGHEST
MASKED = -1e30
ROOT_TWO_PI = math.sqrt(2.0 / math.pi)


def gelu_tanh(inputs):
    return (
        0.5
        * inputs
        * (1.0 + jnp.tanh(ROOT_TWO_PI * (inputs + 0.044715 * inputs * inputs * inputs)))
    )


def gated(gate_pre, up_pre):
    return gelu_tanh(gate_pre) * up_pre


def project(value_vectors, weight_matrix):
    return jnp.einsum(
        "gzk,kp->gzp", value_vectors, weight_matrix, preferred_element_type=jnp.float32
    )


def project_back(incoming_gradient, weight_matrix):
    return jnp.einsum(
        "qzk,jk->qzj", incoming_gradient, weight_matrix, preferred_element_type=jnp.float32
    )


def weight_grad(value_vectors, incoming_gradient):
    return jnp.einsum(
        "rbm,rbc->mc", value_vectors, incoming_gradient, preferred_element_type=jnp.float32
    )


def split_heads(value_vectors):
    return value_vectors.reshape(
        value_vectors.shape[0], value_vectors.shape[1], value_vectors.shape[2] // HEAD, HEAD
    )


def norm_forward(value_vectors, gain_vec):
    local_sum = jnp.sum(value_vectors * value_vectors, axis=-1)
    row_total = lax.psum(local_sum, "col")
    inv_rms = lax.rsqrt(row_total / D + EPSILON)[..., None]
    return (value_vectors * inv_rms * gain_vec, inv_rms)


def norm_backward(value_vectors, inv_rms, gain_vec, incoming_gradient):
    local_sum = jnp.sum(incoming_gradient * gain_vec * value_vectors, axis=-1)
    row_total = lax.psum(local_sum, "col")
    input_grad = incoming_gradient * gain_vec * inv_rms - value_vectors * (
        inv_rms * inv_rms * inv_rms
    ) * (row_total[..., None] / D)
    return (input_grad, jnp.sum(incoming_gradient * value_vectors * inv_rms, axis=(0, 1)))


def widen(value_vectors):
    return lax.all_gather(value_vectors.astype(jnp.bfloat16), "col", axis=2, tiled=True)


def narrow(partial_rows):
    return lax.psum_scatter(partial_rows, "col", scatter_dimension=2, tiled=True)


def widen_grad(incoming_gradient):
    return lax.all_gather(incoming_gradient.astype(jnp.bfloat16), "col", axis=2, tiled=True)


def narrow_grad(partial_rows):
    return lax.psum_scatter(partial_rows, "col", scatter_dimension=2, tiled=True)


def bias_blocks(vector, length):
    block_rows = min(512, length)
    block_count = length // block_rows
    head_count = vector.shape[0]
    padded = jnp.pad(vector, ((0, 0), (0, 1)))
    tables = []
    for block_idx in range(block_count):
        first = block_idx * block_rows
        window = padded[:, length - first - block_rows : 2 * length - first]
        tiled = jnp.broadcast_to(
            window[:, None, :], (head_count, block_rows, length + block_rows)
        ).reshape(head_count, -1)
        skewed = tiled[:, block_rows - 1 : block_rows - 1 + block_rows * (length + block_rows - 1)]
        tables.append(
            skewed.reshape(head_count, block_rows, length + block_rows - 1)[:, :, :length]
        )
    return jnp.stack(tables, axis=0)


def self_mask(rel_blocks):

    def apply(scores, start_row, context):
        starts, lengths = context
        head_count, block_rows, key_count = scores.shape
        row_ids = start_row + jnp.arange(block_rows, dtype=jnp.int32)
        column_positions = jnp.arange(key_count, dtype=jnp.int32)
        rel_bias = lax.dynamic_index_in_dim(rel_blocks, start_row // block_rows, 0, keepdims=False)
        piece_ends = starts + lengths
        row_in = (row_ids[None, :] >= starts[:, None]) & (row_ids[None, :] < piece_ends[:, None])
        col_in = (column_positions[None, :] >= starts[:, None]) & (
            column_positions[None, :] < piece_ends[:, None]
        )
        inside = jnp.any(row_in[:, :, None] & col_in[:, None, :], axis=0)
        allowed = inside | (column_positions[None, :] <= row_ids[:, None])
        return jnp.where(allowed[None], scores + rel_bias, MASKED)

    return apply


def open_mask(scores, start_row, context):
    return scores


def diagonal_sums(dscores, start_row):
    head_count, block_rows, key_count = dscores.shape
    shifted = jnp.pad(dscores, ((0, 0), (0, 0), (block_rows - 1, 0))).reshape(head_count, -1)
    shifted = jnp.pad(shifted, ((0, 0), (0, block_rows)))
    sums = jnp.sum(shifted.reshape(head_count, block_rows, key_count + block_rows), axis=1)[
        :, : key_count + block_rows - 1
    ]
    placed = jnp.zeros((head_count, 2 * key_count - 1), jnp.float32)
    return lax.dynamic_update_slice_in_dim(placed, sums, key_count - start_row - block_rows, 1)


def attend_forward(queries, key_rows, value_rows, context, masking):
    seq_count, length, head_count, head_width = queries.shape
    block_rows = min(512, length)
    starts = jnp.arange(length // block_rows, dtype=jnp.int32) * block_rows

    def per_sequence(seq_item):
        seq_queries, seq_keys, seq_values, seq_context = seq_item

        def per_block(start_row):
            query_block = lax.dynamic_slice_in_dim(seq_queries, start_row, block_rows, 0)
            scores = jnp.einsum(
                "qhd,khd->hqk", query_block, seq_keys, preferred_element_type=jnp.float32
            )
            scores = masking(scores, start_row, seq_context)
            row_max = jnp.max(scores, axis=-1, keepdims=True)
            exp_scores = jnp.exp(scores - row_max)
            row_total = jnp.sum(exp_scores, axis=-1, keepdims=True)
            softmax_w = (exp_scores / row_total).astype(jnp.bfloat16)
            mixed_rows = jnp.einsum(
                "hqk,khd->qhd", softmax_w, seq_values, preferred_element_type=jnp.float32
            )
            return (mixed_rows.astype(jnp.bfloat16), (row_max + jnp.log(row_total))[..., 0])

        mixed_rows, log_normalizer = lax.map(per_block, starts)
        return (mixed_rows.reshape(length, head_count * head_width), log_normalizer)

    return lax.map(per_sequence, (queries, key_rows, value_rows, context))


def attend_backward(
    queries, key_rows, value_rows, log_normalizer, grads, context, masking, span_sums
):
    seq_count, length, head_count, head_width = queries.shape
    key_count = key_rows.shape[1]
    block_rows = min(512, length)
    starts = jnp.arange(length // block_rows, dtype=jnp.int32) * block_rows

    def per_sequence(seq_item):
        seq_queries, seq_keys, seq_values, sequence_log_normalizer, seq_grads, seq_context = (
            seq_item
        )

        def per_block(carried, step_item):
            key_acc, value_acc, diag_acc = carried
            start_row, block_logsum = step_item
            query_block = lax.dynamic_slice_in_dim(seq_queries, start_row, block_rows, 0)
            grad_block = lax.dynamic_slice_in_dim(seq_grads, start_row, block_rows, 0)
            scores = jnp.einsum(
                "qhd,khd->hqk", query_block, seq_keys, preferred_element_type=jnp.float32
            )
            scores = masking(scores, start_row, seq_context)
            softmax_w = jnp.exp(scores - block_logsum[..., None])
            dprobs = jnp.einsum(
                "qhd,khd->hqk", grad_block, seq_values, preferred_element_type=jnp.float32
            )
            dscores = softmax_w * (dprobs - jnp.sum(softmax_w * dprobs, axis=-1, keepdims=True))
            low_scores = dscores.astype(jnp.bfloat16)
            query_grad = jnp.einsum(
                "hqk,khd->qhd", low_scores, seq_keys, preferred_element_type=jnp.float32
            )
            key_acc = key_acc + jnp.einsum(
                "hqk,qhd->khd", low_scores, query_block, preferred_element_type=jnp.float32
            )
            value_acc = value_acc + jnp.einsum(
                "hqk,qhd->khd",
                softmax_w.astype(jnp.bfloat16),
                grad_block,
                preferred_element_type=jnp.float32,
            )
            if span_sums:
                diag_acc = diag_acc + diagonal_sums(dscores, start_row)
            return ((key_acc, value_acc, diag_acc), query_grad)

        initial = (
            jnp.zeros((key_count, head_count, head_width), jnp.float32),
            jnp.zeros((key_count, head_count, head_width), jnp.float32),
            jnp.zeros((head_count, 2 * key_count - 1), jnp.float32),
        )
        (key_acc, value_acc, diag_acc), query_grad = lax.scan(
            per_block, initial, (starts, sequence_log_normalizer)
        )
        return (
            query_grad.reshape(length, head_count * head_width),
            key_acc.reshape(key_count, head_count * head_width),
            value_acc.reshape(key_count, head_count * head_width),
            diag_acc,
        )

    return lax.map(per_sequence, (queries, key_rows, value_rows, log_normalizer, grads, context))


def body(
    hidden_in,
    encoded,
    cotangent,
    piece_start,
    image_piece_lengths,
    bucket_table,
    self_query,
    self_key,
    self_value,
    self_out,
    rel_weight,
    cross_query,
    cross_key,
    cross_value,
    cross_out,
    ffn_gate,
    ffn_up,
    ffn_down,
    gain_self,
    gain_cross,
    gain_ffn,
    gain_final,
):
    onehot = (bucket_table[:, None] == jnp.arange(BUCKETS, dtype=jnp.int32)[None, :]).astype(
        jnp.float32
    )
    batch_seqs = hidden_in.shape[0] // MB
    length = hidden_in.shape[1]
    row_totals = None
    gain_totals = None
    out_list = []
    input_list = []
    encoded_list = []
    for batch_idx in range(MB):
        lower = batch_idx * batch_seqs
        upper = lower + batch_seqs
        weights = (
            lax.all_gather(self_query, "row", axis=0, tiled=True),
            lax.all_gather(self_key, "row", axis=0, tiled=True),
            lax.all_gather(self_value, "row", axis=0, tiled=True),
            lax.all_gather(self_out, "row", axis=1, tiled=True),
            lax.all_gather(rel_weight, "row", axis=0, tiled=True),
            lax.all_gather(cross_query, "row", axis=0, tiled=True),
            lax.all_gather(cross_key, "row", axis=0, tiled=True),
            lax.all_gather(cross_value, "row", axis=0, tiled=True),
            lax.all_gather(cross_out, "row", axis=1, tiled=True),
            lax.all_gather(ffn_gate, "row", axis=0, tiled=True),
            lax.all_gather(ffn_up, "row", axis=0, tiled=True),
            lax.all_gather(ffn_down, "row", axis=1, tiled=True),
        )
        (
            w_query,
            w_key,
            w_value,
            w_out,
            w_rel,
            c_query,
            c_key,
            c_value,
            c_out,
            f_gate,
            f_up,
            f_down,
        ) = weights
        inputs = hidden_in[lower:upper].astype(jnp.float32)
        enc_rows = encoded[lower:upper]
        grad_out = cotangent[lower:upper].astype(jnp.float32)
        context = (piece_start[lower:upper], image_piece_lengths[lower:upper])
        vector = jnp.dot(onehot, w_rel.astype(jnp.float32), precision=PRECISE).T
        self_masking = self_mask(bias_blocks(vector, length))
        normed_one, scale_one = norm_forward(inputs, gain_self)
        full_one = widen(normed_one)
        queries = split_heads(project(full_one, w_query).astype(jnp.bfloat16))
        key_rows = split_heads(project(full_one, w_key).astype(jnp.bfloat16))
        value_rows = split_heads(project(full_one, w_value).astype(jnp.bfloat16))
        mixed_one, logsum_one = attend_forward(queries, key_rows, value_rows, context, self_masking)
        first_sum = inputs + narrow(project(mixed_one, w_out))
        normed_two, scale_two = norm_forward(first_sum, gain_cross)
        full_two = widen(normed_two)
        enc_full = widen(enc_rows)
        cross_q = split_heads(project(full_two, c_query).astype(jnp.bfloat16))
        cross_k = split_heads(project(enc_full, c_key).astype(jnp.bfloat16))
        cross_v = split_heads(project(enc_full, c_value).astype(jnp.bfloat16))
        mixed_two, logsum_two = attend_forward(cross_q, cross_k, cross_v, context, open_mask)
        second_sum = first_sum + narrow(project(mixed_two, c_out))
        normed_three, scale_three = norm_forward(second_sum, gain_ffn)
        full_three = widen(normed_three)
        gate_pre = project(full_three, f_gate)
        up_pre = project(full_three, f_up)
        hidden_mid = gated(gate_pre, up_pre).astype(jnp.bfloat16)
        third_sum = second_sum + narrow(project(hidden_mid, f_down))
        normed_four, scale_four = norm_forward(third_sum, gain_final)
        out_list.append(normed_four.astype(jnp.bfloat16))
        grad_three, final_gain_grad = norm_backward(third_sum, scale_four, gain_final, grad_out)
        branch_three = widen_grad(grad_three)
        down_grad = weight_grad(hidden_mid, branch_three)
        mid_low = lax.optimization_barrier(project_back(branch_three, f_down).astype(jnp.bfloat16))
        gate_grad, up_grad = jax.vjp(gated, gate_pre, up_pre)[1](mid_low.astype(jnp.float32))
        gate_low = gate_grad.astype(jnp.bfloat16)
        up_low = up_grad.astype(jnp.bfloat16)
        gate_wgrad = weight_grad(full_three, gate_low)
        up_wgrad = weight_grad(full_three, up_low)
        normed_grad_three = narrow_grad(project_back(gate_low, f_gate) + project_back(up_low, f_up))
        back_three, ffn_gain_grad = norm_backward(
            second_sum, scale_three, gain_ffn, normed_grad_three
        )
        grad_two = grad_three + back_three
        branch_two = widen_grad(grad_two)
        cross_out_wgrad = weight_grad(mixed_two, branch_two)
        mixed_grad_two = split_heads(project_back(branch_two, c_out).astype(jnp.bfloat16))
        cq_grad, ck_grad, cv_grad, unused_diag = attend_backward(
            cross_q, cross_k, cross_v, logsum_two, mixed_grad_two, context, open_mask, False
        )
        cq_low = cq_grad.astype(jnp.bfloat16)
        ck_low = ck_grad.astype(jnp.bfloat16)
        cv_low = cv_grad.astype(jnp.bfloat16)
        cq_wgrad = weight_grad(full_two, cq_low)
        ck_wgrad = weight_grad(enc_full, ck_low)
        cv_wgrad = weight_grad(enc_full, cv_low)
        joined = jnp.concatenate(
            [
                project_back(cq_low, c_query),
                project_back(ck_low, c_key) + project_back(cv_low, c_value),
            ],
            axis=1,
        )
        joined = narrow_grad(joined)
        back_two, cross_gain_grad = norm_backward(
            first_sum, scale_two, gain_cross, joined[:, :length]
        )
        encoded_list.append(joined[:, length:])
        grad_one = grad_two + back_two
        branch_one = widen_grad(grad_one)
        self_out_wgrad = weight_grad(mixed_one, branch_one)
        mixed_grad_one = split_heads(project_back(branch_one, w_out).astype(jnp.bfloat16))
        q_grad, k_grad, v_grad, diag_rows = attend_backward(
            queries, key_rows, value_rows, logsum_one, mixed_grad_one, context, self_masking, True
        )
        q_low = q_grad.astype(jnp.bfloat16)
        k_low = k_grad.astype(jnp.bfloat16)
        v_low = v_grad.astype(jnp.bfloat16)
        rel_wgrad = jnp.dot(onehot.T, jnp.sum(diag_rows, axis=0).T, precision=PRECISE)
        query_wgrad = weight_grad(full_one, q_low)
        key_wgrad = weight_grad(full_one, k_low)
        value_wgrad = weight_grad(full_one, v_low)
        normed_grad_one = narrow_grad(
            project_back(q_low, w_query) + project_back(k_low, w_key) + project_back(v_low, w_value)
        )
        back_one, self_gain_grad = norm_backward(inputs, scale_one, gain_self, normed_grad_one)
        input_list.append(grad_one + back_one)
        batch_grads = (
            query_wgrad,
            key_wgrad,
            value_wgrad,
            self_out_wgrad,
            rel_wgrad,
            cq_wgrad,
            ck_wgrad,
            cv_wgrad,
            cross_out_wgrad,
            gate_wgrad,
            up_wgrad,
            down_grad,
        )
        batch_gains = (self_gain_grad, cross_gain_grad, ffn_gain_grad, final_gain_grad)
        gain_totals = (
            batch_gains if gain_totals is None else jax.tree.map(jnp.add, gain_totals, batch_gains)
        )
        reduced = (
            lax.psum_scatter(
                batch_grads[0].astype(jnp.bfloat16), "row", scatter_dimension=0, tiled=True
            ).astype(jnp.float32),
            lax.psum_scatter(
                batch_grads[1].astype(jnp.bfloat16), "row", scatter_dimension=0, tiled=True
            ).astype(jnp.float32),
            lax.psum_scatter(
                batch_grads[2].astype(jnp.bfloat16), "row", scatter_dimension=0, tiled=True
            ).astype(jnp.float32),
            lax.psum_scatter(
                batch_grads[3].astype(jnp.bfloat16), "row", scatter_dimension=1, tiled=True
            ).astype(jnp.float32),
            lax.psum_scatter(
                batch_grads[4].astype(jnp.bfloat16), "row", scatter_dimension=0, tiled=True
            ).astype(jnp.float32),
            lax.psum_scatter(
                batch_grads[5].astype(jnp.bfloat16), "row", scatter_dimension=0, tiled=True
            ).astype(jnp.float32),
            lax.psum_scatter(
                batch_grads[6].astype(jnp.bfloat16), "row", scatter_dimension=0, tiled=True
            ).astype(jnp.float32),
            lax.psum_scatter(
                batch_grads[7].astype(jnp.bfloat16), "row", scatter_dimension=0, tiled=True
            ).astype(jnp.float32),
            lax.psum_scatter(
                batch_grads[8].astype(jnp.bfloat16), "row", scatter_dimension=1, tiled=True
            ).astype(jnp.float32),
            lax.psum_scatter(
                batch_grads[9].astype(jnp.bfloat16), "row", scatter_dimension=0, tiled=True
            ).astype(jnp.float32),
            lax.psum_scatter(
                batch_grads[10].astype(jnp.bfloat16), "row", scatter_dimension=0, tiled=True
            ).astype(jnp.float32),
            lax.psum_scatter(
                batch_grads[11].astype(jnp.bfloat16), "row", scatter_dimension=1, tiled=True
            ).astype(jnp.float32),
        )
        row_totals = reduced if row_totals is None else jax.tree.map(jnp.add, row_totals, reduced)
    gain_sums = lax.psum((gain_totals[0], gain_totals[1], gain_totals[2], gain_totals[3]), "row")
    totals = (
        lax.psum(row_totals[0].astype(jnp.bfloat16), "dp").astype(jnp.float32),
        lax.psum(row_totals[1].astype(jnp.bfloat16), "dp").astype(jnp.float32),
        lax.psum(row_totals[2].astype(jnp.bfloat16), "dp").astype(jnp.float32),
        lax.psum(row_totals[3].astype(jnp.bfloat16), "dp").astype(jnp.float32),
        lax.psum(row_totals[4].astype(jnp.bfloat16), "dp").astype(jnp.float32),
        lax.psum(row_totals[5].astype(jnp.bfloat16), "dp").astype(jnp.float32),
        lax.psum(row_totals[6].astype(jnp.bfloat16), "dp").astype(jnp.float32),
        lax.psum(row_totals[7].astype(jnp.bfloat16), "dp").astype(jnp.float32),
        lax.psum(row_totals[8].astype(jnp.bfloat16), "dp").astype(jnp.float32),
        lax.psum(row_totals[9].astype(jnp.bfloat16), "dp").astype(jnp.float32),
        lax.psum(row_totals[10].astype(jnp.bfloat16), "dp").astype(jnp.float32),
        lax.psum(row_totals[11].astype(jnp.bfloat16), "dp").astype(jnp.float32),
        lax.psum(gain_sums[0].astype(jnp.bfloat16), "dp").astype(jnp.float32),
        lax.psum(gain_sums[1].astype(jnp.bfloat16), "dp").astype(jnp.float32),
        lax.psum(gain_sums[2].astype(jnp.bfloat16), "dp").astype(jnp.float32),
        lax.psum(gain_sums[3].astype(jnp.bfloat16), "dp").astype(jnp.float32),
    )
    return (
        jnp.concatenate(out_list, axis=0),
        jnp.concatenate(input_list, axis=0),
        jnp.concatenate(encoded_list, axis=0),
        totals[0],
        totals[1],
        totals[2],
        totals[3],
        totals[4],
        totals[5],
        totals[6],
        totals[7],
        totals[8],
        totals[9],
        totals[10],
        totals[11],
        totals[12],
        totals[13],
        totals[14],
        totals[15],
    )


def solution(mesh):
    placed = (
        P(("dp", "row"), None, "col"),
        P(("dp", "row"), None, "col"),
        P(("dp", "row"), None, "col"),
        P(("dp", "row"), None),
        P(("dp", "row"), None),
        P(),
        P("row", "col"),
        P("row", "col"),
        P("row", "col"),
        P("col", "row"),
        P("row", "col"),
        P("row", "col"),
        P("row", "col"),
        P("row", "col"),
        P("col", "row"),
        P("row", "col"),
        P("row", "col"),
        P("col", "row"),
        P("col"),
        P("col"),
        P("col"),
        P("col"),
    )
    return jax.shard_map(
        body,
        mesh=mesh,
        in_specs=placed,
        out_specs=(
            P(("dp", "row"), None, "col"),
            P(("dp", "row"), None, "col"),
            P(("dp", "row"), None, "col"),
            P("row", "col"),
            P("row", "col"),
            P("row", "col"),
            P("col", "row"),
            P("row", "col"),
            P("row", "col"),
            P("row", "col"),
            P("row", "col"),
            P("col", "row"),
            P("row", "col"),
            P("row", "col"),
            P("col", "row"),
            P("col"),
            P("col"),
            P("col"),
            P("col"),
        ),
        check_vma=False,
    )
```

profile of v0, /device:TPU:0, one launch (start us, length us, event | category | flops | bytes accessed | tf_op | source)
XLA Modules:
  0.0 3865.5 jit_solution(14675109285661560477)
XLA Ops:
  138.1 341.4 %while.224 = (u32[]{:T(128)}, f32[1,6,785920]{2,1,0:T(8,128)}, f32[4715520]{0:T(1024)}, u32[]{}, f32[]{:T(128)}, /*index=5*/u32[]{}, u32[]{}, u32[]{}) while((u32[]{:T(128)}, f32[1,6,785920]{2,1,0:T(8,128)}, f32[4715520]{0:T(1024)}, u32[]{}, f32[]{:T(128)}, /*index=5*/u32[]{}, u32[]{}, u32[]{}) %tuple.328), condition=%wide.cond.2, body=%wide.body.2.sunk | while | flops 9 | bytes 12574921
  138.7 30.0 dynamic-slice_reduce_fusion.4
  195.6 30.0 dynamic-slice_reduce_fusion.4
  225.6 26.4 dynamic-update-slice.22
  252.6 30.0 dynamic-slice_reduce_fusion.4
  282.6 26.4 dynamic-update-slice.22
  309.6 30.0 dynamic-slice_reduce_fusion.4
  339.6 26.5 dynamic-update-slice.22
  366.6 30.0 dynamic-slice_reduce_fusion.4
  396.6 26.5 dynamic-update-slice.22
  423.6 30.0 dynamic-slice_reduce_fusion.4
  479.6 29.4 reshape.1507
  550.0 341.6 %while.225 = (u32[]{:T(128)}, f32[1,6,785920]{2,1,0:T(8,128)}, f32[4715520]{0:T(1024)}, u32[]{}, f32[]{:T(128)}, /*index=5*/u32[]{}, u32[]{}, u32[]{}) while((u32[]{:T(128)}, f32[1,6,785920]{2,1,0:T(8,128)}, f32[4715520]{0:T(1024)}, u32[]{}, f32[]{:T(128)}, /*index=5*/u32[]{}, u32[]{}, u32[]{}) %tuple.331), condition=%wide.cond.3, body=%wide.body.3.sunk | while | flops 9 | bytes 12574921
  550.7 30.0 dynamic-slice_reduce_fusion.5
  580.8 26.4 dynamic-update-slice.23
  607.7 30.0 dynamic-slice_reduce_fusion.5
  637.7 26.4 dynamic-update-slice.23
  664.7 30.0 dynamic-slice_reduce_fusion.5
  694.7 26.4 dynamic-update-slice.23
  721.7 30.0 dynamic-slice_reduce_fusion.5
  751.7 26.4 dynamic-update-slice.23
  778.7 30.0 dynamic-slice_reduce_fusion.5
  808.7 26.4 dynamic-update-slice.23
  835.7 30.0 dynamic-slice_reduce_fusion.5
  891.6 29.3 reshape.1505
  957.4 40.3 %while.216 = (s32[]{:T(128)}, bf16[2,512,6,64]{1,3,2,0:T(8,128)(2,1)}, f32[2,6,512]{2,1,0:T(8,128)}, s32[2]{0:T(128)S(1)}, s32[2]{0:T(128)S(1)}, /*index=5*/s32[...) while((s32[]{:T(128)}, ...), condition=%wide.region_26.27_spmd, body=%wide.region_22.26_spmd.sunk | while | flops 833296896 | bytes 61407780 | solution.py:165
  1008.5 37.8 while.214
  1253.7 33.9 all-gather.24.cloned.1.call-done
  1295.7 29.2 all-gather.26.cloned.1.call-done
  1608.0 983.5 %while.220 = (s32[]{:T(128)}, f32[1024,6,64]{0,2,1:T(8,128)}, f32[1024,6,64]{0,2,1:T(8,128)}, f32[6,2047]{1,0:T(8,128)S(1)}, bf16[2,512,6,64]{1,3,2,0:T(8,128)(2...) while((s32[]{:T(128)}, f32[1024,6,64]{0,2,1:T(8,128)}, ...), condition=%wide.region_55.56_spmd.clone, body=%wide.region_51.55_spmd.clone.sunk | while | flops 2053642752 | bytes 412849088 | solution.py:220
  1662.3 28.3 reshape.1555
  1690.6 389.7 %while.226 = (u32[]{:T(128)}, f32[4715520]{0:T(1024)}, f32[1,6,785920]{2,1,0:T(8,128)}, u32[]{}, u32[]{}, /*index=5*/u32[]{}, u32[]{}, u32[]{}) while((u32[]{:T(128)}, f32[4715520]{0:T(1024)}, f32[1,6,785920]{2,1,0:T(8,128)}, u32[]{}, u32[]{}, /*index=5*/u32[]{}, u32[]{}, u32[]{}) %tuple.325), condition=%wide.cond, body=%wide.body.sunk | while | flops 9 | bytes 18862264
  1696.4 59.2 %dynamic-update-slice.25 = f32[1,6,785920]{2,1,0:T(8,128)} dynamic-update-slice(f32[1,6,785920]{2,1,0:T(8,128)} %get-tuple-element.2567, f32[1,1,785920]{2,1,0:T(1,128)S(1)} %reshape.1558, u32[]{:T(128)S(6)} %multiply.112, u32[]{:T(128)S(6)} %multiply.114, u32[]{} %constant.925..sunk2) | dynamic-update-slice | bytes 6287364
  1761.4 59.2 %dynamic-update-slice.25 = f32[1,6,785920]{2,1,0:T(8,128)} dynamic-update-slice(f32[1,6,785920]{2,1,0:T(8,128)} %get-tuple-element.2567, f32[1,1,785920]{2,1,0:T(1,128)S(1)} %reshape.1558, u32[]{:T(128)S(6)} %multiply.112, u32[]{:T(128)S(6)} %multiply.114, u32[]{} %constant.925..sunk2) | dynamic-update-slice | bytes 6287364
  1826.4 59.2 %dynamic-update-slice.25 = f32[1,6,785920]{2,1,0:T(8,128)} dynamic-update-slice(f32[1,6,785920]{2,1,0:T(8,128)} %get-tuple-element.2567, f32[1,1,785920]{2,1,0:T(1,128)S(1)} %reshape.1558, u32[]{:T(128)S(6)} %multiply.112, u32[]{:T(128)S(6)} %multiply.114, u32[]{} %constant.925..sunk2) | dynamic-update-slice | bytes 6287364
  1891.4 59.2 %dynamic-update-slice.25 = f32[1,6,785920]{2,1,0:T(8,128)} dynamic-update-slice(f32[1,6,785920]{2,1,0:T(8,128)} %get-tuple-element.2567, f32[1,1,785920]{2,1,0:T(1,128)S(1)} %reshape.1558, u32[]{:T(128)S(6)} %multiply.112, u32[]{:T(128)S(6)} %multiply.114, u32[]{} %constant.925..sunk2) | dynamic-update-slice | bytes 6287364
  1956.3 59.1 %dynamic-update-slice.25 = f32[1,6,785920]{2,1,0:T(8,128)} dynamic-update-slice(f32[1,6,785920]{2,1,0:T(8,128)} %get-tuple-element.2567, f32[1,1,785920]{2,1,0:T(1,128)S(1)} %reshape.1558, u32[]{:T(128)S(6)} %multiply.112, u32[]{:T(128)S(6)} %multiply.114, u32[]{} %constant.925..sunk2) | dynamic-update-slice | bytes 6287364
  2021.3 59.1 %dynamic-update-slice.25 = f32[1,6,785920]{2,1,0:T(8,128)} dynamic-update-slice(f32[1,6,785920]{2,1,0:T(8,128)} %get-tuple-element.2567, f32[1,1,785920]{2,1,0:T(1,128)S(1)} %reshape.1558, u32[]{:T(128)S(6)} %multiply.112, u32[]{:T(128)S(6)} %multiply.114, u32[]{} %constant.925..sunk2) | dynamic-update-slice | bytes 6287364
  2154.1 28.3 reshape.1555
  2182.3 389.2 %while.226 = (u32[]{:T(128)}, f32[4715520]{0:T(1024)}, f32[1,6,785920]{2,1,0:T(8,128)}, u32[]{}, u32[]{}, /*index=5*/u32[]{}, u32[]{}, u32[]{}) while((u32[]{:T(128)}, f32[4715520]{0:T(1024)}, f32[1,6,785920]{2,1,0:T(8,128)}, u32[]{}, u32[]{}, /*index=5*/u32[]{}, u32[]{}, u32[]{}) %tuple.325), condition=%wide.cond, body=%wide.body.sunk | while | flops 9 | bytes 18862264
  2188.1 59.1 %dynamic-update-slice.25 = f32[1,6,785920]{2,1,0:T(8,128)} dynamic-update-slice(f32[1,6,785920]{2,1,0:T(8,128)} %get-tuple-element.2567, f32[1,1,785920]{2,1,0:T(1,128)S(1)} %reshape.1558, u32[]{:T(128)S(6)} %multiply.112, u32[]{:T(128)S(6)} %multiply.114, u32[]{} %constant.925..sunk2) | dynamic-update-slice | bytes 6287364
  2253.0 59.1 %dynamic-update-slice.25 = f32[1,6,785920]{2,1,0:T(8,128)} dynamic-update-slice(f32[1,6,785920]{2,1,0:T(8,128)} %get-tuple-element.2567, f32[1,1,785920]{2,1,0:T(1,128)S(1)} %reshape.1558, u32[]{:T(128)S(6)} %multiply.112, u32[]{:T(128)S(6)} %multiply.114, u32[]{} %constant.925..sunk2) | dynamic-update-slice | bytes 6287364
  2317.9 59.1 %dynamic-update-slice.25 = f32[1,6,785920]{2,1,0:T(8,128)} dynamic-update-slice(f32[1,6,785920]{2,1,0:T(8,128)} %get-tuple-element.2567, f32[1,1,785920]{2,1,0:T(1,128)S(1)} %reshape.1558, u32[]{:T(128)S(6)} %multiply.112, u32[]{:T(128)S(6)} %multiply.114, u32[]{} %constant.925..sunk2) | dynamic-update-slice | bytes 6287364
  2382.7 59.1 %dynamic-update-slice.25 = f32[1,6,785920]{2,1,0:T(8,128)} dynamic-update-slice(f32[1,6,785920]{2,1,0:T(8,128)} %get-tuple-element.2567, f32[1,1,785920]{2,1,0:T(1,128)S(1)} %reshape.1558, u32[]{:T(128)S(6)} %multiply.112, u32[]{:T(128)S(6)} %multiply.114, u32[]{} %constant.925..sunk2) | dynamic-update-slice | bytes 6287364
  2447.6 59.1 %dynamic-update-slice.25 = f32[1,6,785920]{2,1,0:T(8,128)} dynamic-update-slice(f32[1,6,785920]{2,1,0:T(8,128)} %get-tuple-element.2567, f32[1,1,785920]{2,1,0:T(1,128)S(1)} %reshape.1558, u32[]{:T(128)S(6)} %multiply.112, u32[]{:T(128)S(6)} %multiply.114, u32[]{} %constant.925..sunk2) | dynamic-update-slice | bytes 6287364
  2512.5 59.1 %dynamic-update-slice.25 = f32[1,6,785920]{2,1,0:T(8,128)} dynamic-update-slice(f32[1,6,785920]{2,1,0:T(8,128)} %get-tuple-element.2567, f32[1,1,785920]{2,1,0:T(1,128)S(1)} %reshape.1558, u32[]{:T(128)S(6)} %multiply.112, u32[]{:T(128)S(6)} %multiply.114, u32[]{} %constant.925..sunk2) | dynamic-update-slice | bytes 6287364
  2600.7 997.8 %while.223 = (s32[]{:T(128)}, f32[1024,6,64]{0,2,1:T(8,128)}, f32[1024,6,64]{0,2,1:T(8,128)}, f32[6,2047]{1,0:T(8,128)S(1)}, bf16[2,512,6,64]{1,3,2,0:T(8,128)(2...) while((s32[]{:T(128)}, f32[1024,6,64]{0,2,1:T(8,128)}, ...), condition=%wide.region_74.75_spmd.clone, body=%wide.region_70.74_spmd.clone.sunk | while | flops 2053642752 | bytes 412849088 | solution.py:220
  2662.3 28.3 reshape.1556
  2690.6 389.2 %while.227 = (u32[]{:T(128)}, f32[4715520]{0:T(1024)}, f32[1,6,785920]{2,1,0:T(8,128)}, u32[]{}, u32[]{}, /*index=5*/u32[]{}, u32[]{}, u32[]{}) while((u32[]{:T(128)}, f32[4715520]{0:T(1024)}, f32[1,6,785920]{2,1,0:T(8,128)}, u32[]{}, u32[]{}, /*index=5*/u32[]{}, u32[]{}, u32[]{}) %tuple.322), condition=%wide.cond.1, body=%wide.body.1.sunk | while | flops 9 | bytes 18862264
  2696.4 59.1 %dynamic-update-slice.24 = f32[1,6,785920]{2,1,0:T(8,128)} dynamic-update-slice(f32[1,6,785920]{2,1,0:T(8,128)} %get-tuple-element.2543, f32[1,1,785920]{2,1,0:T(1,128)S(1)} %reshape.1557, u32[]{:T(128)S(6)} %multiply.108, u32[]{:T(128)S(6)} %multiply.110, u32[]{} %constant.925..sunk.1..sunk) | dynamic-update-slice | bytes 6287364
  2761.2 59.1 %dynamic-update-slice.24 = f32[1,6,785920]{2,1,0:T(8,128)} dynamic-update-slice(f32[1,6,785920]{2,1,0:T(8,128)} %get-tuple-element.2543, f32[1,1,785920]{2,1,0:T(1,128)S(1)} %reshape.1557, u32[]{:T(128)S(6)} %multiply.108, u32[]{:T(128)S(6)} %multiply.110, u32[]{} %constant.925..sunk.1..sunk) | dynamic-update-slice | bytes 6287364
  2826.1 59.1 %dynamic-update-slice.24 = f32[1,6,785920]{2,1,0:T(8,128)} dynamic-update-slice(f32[1,6,785920]{2,1,0:T(8,128)} %get-tuple-element.2543, f32[1,1,785920]{2,1,0:T(1,128)S(1)} %reshape.1557, u32[]{:T(128)S(6)} %multiply.108, u32[]{:T(128)S(6)} %multiply.110, u32[]{} %constant.925..sunk.1..sunk) | dynamic-update-slice | bytes 6287364
  2891.0 59.1 %dynamic-update-slice.24 = f32[1,6,785920]{2,1,0:T(8,128)} dynamic-update-slice(f32[1,6,785920]{2,1,0:T(8,128)} %get-tuple-element.2543, f32[1,1,785920]{2,1,0:T(1,128)S(1)} %reshape.1557, u32[]{:T(128)S(6)} %multiply.108, u32[]{:T(128)S(6)} %multiply.110, u32[]{} %constant.925..sunk.1..sunk) | dynamic-update-slice | bytes 6287364
  2955.8 59.1 %dynamic-update-slice.24 = f32[1,6,785920]{2,1,0:T(8,128)} dynamic-update-slice(f32[1,6,785920]{2,1,0:T(8,128)} %get-tuple-element.2543, f32[1,1,785920]{2,1,0:T(1,128)S(1)} %reshape.1557, u32[]{:T(128)S(6)} %multiply.108, u32[]{:T(128)S(6)} %multiply.110, u32[]{} %constant.925..sunk.1..sunk) | dynamic-update-slice | bytes 6287364
  3020.7 59.1 %dynamic-update-slice.24 = f32[1,6,785920]{2,1,0:T(8,128)} dynamic-update-slice(f32[1,6,785920]{2,1,0:T(8,128)} %get-tuple-element.2543, f32[1,1,785920]{2,1,0:T(1,128)S(1)} %reshape.1557, u32[]{:T(128)S(6)} %multiply.108, u32[]{:T(128)S(6)} %multiply.110, u32[]{} %constant.925..sunk.1..sunk) | dynamic-update-slice | bytes 6287364
  3153.5 28.3 reshape.1556
  3181.7 389.2 %while.227 = (u32[]{:T(128)}, f32[4715520]{0:T(1024)}, f32[1,6,785920]{2,1,0:T(8,128)}, u32[]{}, u32[]{}, /*index=5*/u32[]{}, u32[]{}, u32[]{}) while((u32[]{:T(128)}, f32[4715520]{0:T(1024)}, f32[1,6,785920]{2,1,0:T(8,128)}, u32[]{}, u32[]{}, /*index=5*/u32[]{}, u32[]{}, u32[]{}) %tuple.322), condition=%wide.cond.1, body=%wide.body.1.sunk | while | flops 9 | bytes 18862264
  3187.6 59.1 %dynamic-update-slice.24 = f32[1,6,785920]{2,1,0:T(8,128)} dynamic-update-slice(f32[1,6,785920]{2,1,0:T(8,128)} %get-tuple-element.2543, f32[1,1,785920]{2,1,0:T(1,128)S(1)} %reshape.1557, u32[]{:T(128)S(6)} %multiply.108, u32[]{:T(128)S(6)} %multiply.110, u32[]{} %constant.925..sunk.1..sunk) | dynamic-update-slice | bytes 6287364
  3252.4 59.1 %dynamic-update-slice.24 = f32[1,6,785920]{2,1,0:T(8,128)} dynamic-update-slice(f32[1,6,785920]{2,1,0:T(8,128)} %get-tuple-element.2543, f32[1,1,785920]{2,1,0:T(1,128)S(1)} %reshape.1557, u32[]{:T(128)S(6)} %multiply.108, u32[]{:T(128)S(6)} %multiply.110, u32[]{} %constant.925..sunk.1..sunk) | dynamic-update-slice | bytes 6287364
  3317.3 59.1 %dynamic-update-slice.24 = f32[1,6,785920]{2,1,0:T(8,128)} dynamic-update-slice(f32[1,6,785920]{2,1,0:T(8,128)} %get-tuple-element.2543, f32[1,1,785920]{2,1,0:T(1,128)S(1)} %reshape.1557, u32[]{:T(128)S(6)} %multiply.108, u32[]{:T(128)S(6)} %multiply.110, u32[]{} %constant.925..sunk.1..sunk) | dynamic-update-slice | bytes 6287364
  3382.1 59.1 %dynamic-update-slice.24 = f32[1,6,785920]{2,1,0:T(8,128)} dynamic-update-slice(f32[1,6,785920]{2,1,0:T(8,128)} %get-tuple-element.2543, f32[1,1,785920]{2,1,0:T(1,128)S(1)} %reshape.1557, u32[]{:T(128)S(6)} %multiply.108, u32[]{:T(128)S(6)} %multiply.110, u32[]{} %constant.925..sunk.1..sunk) | dynamic-update-slice | bytes 6287364
  3447.0 59.1 %dynamic-update-slice.24 = f32[1,6,785920]{2,1,0:T(8,128)} dynamic-update-slice(f32[1,6,785920]{2,1,0:T(8,128)} %get-tuple-element.2543, f32[1,1,785920]{2,1,0:T(1,128)S(1)} %reshape.1557, u32[]{:T(128)S(6)} %multiply.108, u32[]{:T(128)S(6)} %multiply.110, u32[]{} %constant.925..sunk.1..sunk) | dynamic-update-slice | bytes 6287364
  3511.9 59.1 %dynamic-update-slice.24 = f32[1,6,785920]{2,1,0:T(8,128)} dynamic-update-slice(f32[1,6,785920]{2,1,0:T(8,128)} %get-tuple-element.2543, f32[1,1,785920]{2,1,0:T(1,128)S(1)} %reshape.1557, u32[]{:T(128)S(6)} %multiply.108, u32[]{:T(128)S(6)} %multiply.110, u32[]{} %constant.925..sunk.1..sunk) | dynamic-update-slice | bytes 6287364
  3753.1 41.5 %all-reduce.21.cloned.1.call-done = (bf16[192,384]{0,1:T(8,128)(2,1)}, bf16[192,384]{0,1:T(8,128)(2,1)}, bf16[192,384]{1,0:T(8,128)(2,1)}, bf16[192,384]{1,0:T(8...) async-done(((bf16[192,384]{0,1:T(8,128)(2,1)}, ...) | async-done | bytes 2359312 | tf_op jit(solution)/shard_map/psum | solution.py:449
  (1098 shorter events, 1542.8 us)
Async XLA Ops:
  8.0 943.5 %all-gather.28.cloned.1.call-start = ((), (), s32[]{:S(2)}) async-start(), calls=%async_computation.43 | async-start | bytes 2359296 | tf_op jit(solution)/shard_map/all_gather | solution.py:73
  14.4 15.5 copy-start.143
  14.4 32.6 copy-start.144
  14.4 49.7 %copy-start.145 = (bf16[192,384]{1,0:T(8,128)(2,1)S(1)}, bf16[192,384]{1,0:T(8,128)(2,1)}, u32[]{:S(2)}) copy-start(bf16[192,384]{1,0:T(8,128)(2,1)} %param.46) | copy-start | bytes 442372
  14.4 989.9 %all-gather.16.cloned.1.call-start = ((), (), s32[]{:S(2)}) async-start(), calls=%async_computation.34 | async-start | bytes 2359296 | tf_op jit(solution)/shard_map/all_gather | solution.py:73
  14.5 65.8 %copy-start.146 = (bf16[384,192]{0,1:T(8,128)(2,1)S(1)}, bf16[384,192]{0,1:T(8,128)(2,1)}, u32[]{:S(2)}) copy-start(bf16[384,192]{0,1:T(8,128)(2,1)} %param.47) | copy-start | bytes 442372
  15.2 1036.3 %reduce-scatter.49.cloned.1.call-start = ((), (), s32[]{:S(2)}) async-start(), calls=%async_computation.44 | async-start | bytes 4718592 | tf_op jit(solution)/shard_map/reduce_scatter | solution.py:77
  933.4 18.2 copy-start.53
  1004.3 59.6 %reduce-scatter.43.cloned.1.call-start = ((), (), s32[]{:S(2)}) async-start(), calls=%async_computation.35 | async-start | bytes 4718592 | tf_op jit(solution)/shard_map/reduce_scatter | solution.py:77
  1051.4 18.5 copy-start.159
  1051.4 95.2 %all-gather.18.cloned.1.call-start = ((), (), s32[]{:S(2)}) async-start(), calls=%async_computation.36 | async-start | bytes 2359296 | tf_op jit(solution)/shard_map/all_gather | solution.py:73
  1067.3 131.1 %copy-start.21 = (f32[1,1024,384]{2,1,0:T(8,128)}, f32[1,1024,384]{2,1,0:T(8,128)S(1)}, u32[]{:S(2)}) copy-start(f32[1,1024,384]{2,1,0:T(8,128)S(1)} %get-tuple-element.1848) | copy-start | bytes 4718596
  1072.9 101.6 %all-gather.30.cloned.1.call-start = ((), (), s32[]{:S(2)}) async-start(), calls=%async_computation.45 | async-start | bytes 2359296 | tf_op jit(solution)/shard_map/all_gather | solution.py:73
  1075.7 35.6 copy-start.42
  1093.1 77.7 %copy-start.32 = (bf16[768,384]{1,0:T(8,128)(2,1)}, bf16[768,384]{1,0:T(8,128)(2,1)S(1)}, u32[]{:S(2)}) copy-start(bf16[768,384]{1,0:T(8,128)(2,1)S(1)} %all_gather.99) | copy-start | bytes 1769476
  1110.3 36.3 copy-start.34
  1146.5 51.9 %reduce-scatter.45.cloned.1.call-start = ((), (), s32[]{:S(2)}) async-start(), calls=%async_computation.37 | async-start | bytes 4718592 | tf_op jit(solution)/shard_map/reduce_scatter | solution.py:77
  1167.8 41.6 %reduce-scatter.51.cloned.1.call-start = ((), (), s32[]{:S(2)}) async-start(), calls=%async_computation.46 | async-start | bytes 4718592 | tf_op jit(solution)/shard_map/reduce_scatter | solution.py:77
  1197.8 39.6 %all-gather.22.cloned.1.call-start = ((), (), s32[]{:S(2)}) async-start(), calls=%async_computation.39 | async-start | bytes 1966080 | tf_op jit(solution)/shard_map/all_gather | solution.py:280
  1198.4 49.6 %all-gather.20.cloned.1.call-start = ((), (), s32[]{:S(2)}) async-start(), calls=%async_computation.38 | async-start | bytes 2359296 | tf_op jit(solution)/shard_map/all_gather | solution.py:73
  1218.4 69.2 %all-gather.24.cloned.1.call-start = ((), (), s32[]{:S(2)}) async-start(), calls=%async_computation.40 | async-start | bytes 1966080 | tf_op jit(solution)/shard_map/all_gather | solution.py:281
  1218.9 106.0 %all-gather.26.cloned.1.call-start = ((), (), s32[]{:S(2)}) async-start(), calls=%async_computation.41 | async-start | bytes 1966080 | tf_op jit(solution)/shard_map/all_gather | solution.py:282
  1219.7 116.0 %all-gather.32.cloned.1.call-start = ((), (), s32[]{:S(2)}) async-start(), calls=%async_computation.47 | async-start | bytes 2359296 | tf_op jit(solution)/shard_map/all_gather | solution.py:73
  1220.4 130.0 %reduce-scatter.47.cloned.1.call-start = ((), (), s32[]{:S(2)}) async-start(), calls=%async_computation.42 | async-start | bytes 4718592 | tf_op jit(solution)/shard_map/reduce_scatter | solution.py:77
  1330.5 34.1 reduce-scatter.53.cloned.1.call-start
  1348.5 48.2 %all-gather.40.cloned.1.call-start = ((), (), s32[]{:S(2)}) async-start(), calls=%async_computation.55 | async-start | bytes 2359296 | tf_op jit(solution)/shard_map/all_gather | solution.py:81
  1385.7 26.2 all-gather.34.cloned.1.call-start
  1386.3 41.2 %reduce-scatter.61.cloned.1.call-start = ((), (), s32[]{:S(2)}) async-start(), calls=%async_computation.56 | async-start | bytes 4718592 | tf_op jit(solution)/shard_map/reduce_scatter | solution.py:85
  1411.8 27.1 reduce-scatter.55.cloned.1.call-start
  1426.8 35.5 all-gather.36.cloned.1.call-start
  1451.2 42.2 %all-gather.42.cloned.1.call-start = ((), (), s32[]{:S(2)}) async-start(), calls=%async_computation.57 | async-start | bytes 2359296 | tf_op jit(solution)/shard_map/all_gather | solution.py:81
  1456.1 66.7 %reduce-scatter.57.cloned.1.call-start = ((), (), s32[]{:S(2)}) async-start(), calls=%async_computation.52 | async-start | bytes 5898240 | tf_op jit(solution)/shard_map/reduce_scatter | solution.py:85
  1492.8 42.6 %reduce-scatter.63.cloned.1.call-start = ((), (), s32[]{:S(2)}) async-start(), calls=%async_computation.58 | async-start | bytes 5898240 | tf_op jit(solution)/shard_map/reduce_scatter | solution.py:85
  1522.2 75.9 %all-gather.38.cloned.1.call-start = ((), (), s32[]{:S(2)}) async-start(), calls=%async_computation.53 | async-start | bytes 2359296 | tf_op jit(solution)/shard_map/all_gather | solution.py:81
  1546.0 55.6 %all-gather.44.cloned.1.call-start = ((), (), s32[]{:S(2)}) async-start(), calls=%async_computation.59 | async-start | bytes 2359296 | tf_op jit(solution)/shard_map/all_gather | solution.py:81
  1546.6 2063.0 %reduce-scatter.99.cloned.1.call-start = ((), (), s32[]{:S(2)}) async-start(), calls=%async_computation.77 | async-start | bytes 1966080 | tf_op jit(solution)/shard_map/reduce_scatter | solution.py:436
  1552.1 2057.6 %reduce-scatter.101.cloned.1.call-start = ((), (), s32[]{:S(2)}) async-start(), calls=%async_computation.78 | async-start | bytes 1966080 | tf_op jit(solution)/shard_map/reduce_scatter | solution.py:436
  1557.9 2058.3 %reduce-scatter.97.cloned.1.call-start = ((), (), s32[]{:S(2)}) async-start(), calls=%async_computation.76 | async-start | bytes 1966080 | tf_op jit(solution)/shard_map/reduce_scatter | solution.py:433
  1562.4 2053.8 %reduce-scatter.95.cloned.1.call-start = ((), (), s32[]{:S(2)}) async-start(), calls=%async_computation.75 | async-start | bytes 1966080 | tf_op jit(solution)/shard_map/reduce_scatter | solution.py:433
  1567.7 2050.6 %reduce-scatter.93.cloned.1.call-start = ((), (), s32[]{:S(2)}) async-start(), calls=%async_computation.74 | async-start | bytes 1966080 | tf_op jit(solution)/shard_map/reduce_scatter | solution.py:430
  1572.4 2045.9 %reduce-scatter.91.cloned.1.call-start = ((), (), s32[]{:S(2)}) async-start(), calls=%async_computation.73 | async-start | bytes 1966080 | tf_op jit(solution)/shard_map/reduce_scatter | solution.py:430
  1578.4 2041.9 %reduce-scatter.109.cloned.1.call-start = ((), (), s32[]{:S(2)}) async-start(), calls=%async_computation.82 | async-start | bytes 737280
  1580.9 2040.5 %reduce-scatter.105.cloned.1.call-start = ((), (), s32[]{:S(2)}) async-start(), calls=%async_computation.80 | async-start | bytes 737280
  1582.4 2040.0 %reduce-scatter.103.cloned.1.call-start = ((), (), s32[]{:S(2)}) async-start(), calls=%async_computation.79 | async-start | bytes 737280
  1583.9 2039.6 %reduce-scatter.107.cloned.1.call-start = ((), (), s32[]{:S(2)}) async-start(), calls=%async_computation.81 | async-start | bytes 737280
  1585.4 2039.2 %reduce-scatter.85.cloned.1.call-start = ((), (), s32[]{:S(2)}) async-start(), calls=%async_computation.70 | async-start | bytes 737280 | tf_op jit(solution)/shard_map/reduce_scatter | solution.py:418
  1588.9 2035.7 %reduce-scatter.83.cloned.1.call-start = ((), (), s32[]{:S(2)}) async-start(), calls=%async_computation.69 | async-start | bytes 737280 | tf_op jit(solution)/shard_map/reduce_scatter | solution.py:418
  1590.9 2040.5 %reduce-scatter.89.cloned.1.call-start = ((), (), s32[]{:S(2)}) async-start(), calls=%async_computation.72 | async-start | bytes 737280 | tf_op jit(solution)/shard_map/reduce_scatter | solution.py:427
  1594.7 2036.8 %reduce-scatter.87.cloned.1.call-start = ((), (), s32[]{:S(2)}) async-start(), calls=%async_computation.71 | async-start | bytes 737280 | tf_op jit(solution)/shard_map/reduce_scatter | solution.py:427
  1598.1 2035.8 %reduce-scatter.79.cloned.1.call-start = ((), (), s32[]{:S(2)}) async-start(), calls=%async_computation.67 | async-start | bytes 737280 | tf_op jit(solution)/shard_map/reduce_scatter | solution.py:412
  1601.5 2032.3 %reduce-scatter.81.cloned.1.call-start = ((), (), s32[]{:S(2)}) async-start(), calls=%async_computation.68 | async-start | bytes 737280 | tf_op jit(solution)/shard_map/reduce_scatter | solution.py:412
  1605.2 2030.3 %reduce-scatter.67.cloned.1.call-start = ((), (), s32[]{:S(2)}) async-start(), calls=%async_computation.61 | async-start | bytes 737280 | tf_op jit(solution)/shard_map/reduce_scatter | solution.py:403
  2596.5 1039.0 %reduce-scatter.69.cloned.1.call-start = ((), (), s32[]{:S(2)}) async-start(), calls=%async_computation.62 | async-start | bytes 737280 | tf_op jit(solution)/shard_map/reduce_scatter | solution.py:403
  3602.6 45.8 %reduce-scatter.71.cloned.1.call-start = ((), (), s32[]{:S(2)}) async-start(), calls=%async_computation.63 | async-start | bytes 737280 | tf_op jit(solution)/shard_map/reduce_scatter | solution.py:406
  3606.0 65.2 %reduce-scatter.73.cloned.1.call-start = ((), (), s32[]{:S(2)}) async-start(), calls=%async_computation.64 | async-start | bytes 737280 | tf_op jit(solution)/shard_map/reduce_scatter | solution.py:406
  3609.6 84.2 %reduce-scatter.75.cloned.1.call-start = ((), (), s32[]{:S(2)}) async-start(), calls=%async_computation.65 | async-start | bytes 737280 | tf_op jit(solution)/shard_map/reduce_scatter | solution.py:409
  3616.1 100.1 %reduce-scatter.77.cloned.1.call-start = ((), (), s32[]{:S(2)}) async-start(), calls=%async_computation.66 | async-start | bytes 737280 | tf_op jit(solution)/shard_map/reduce_scatter | solution.py:409
  3631.3 163.3 %all-reduce.21.cloned.1.call-start = ((), (), s32[]{:S(2)}) async-start(), calls=%async_computation.83 | async-start | bytes 4915200 | tf_op jit(solution)/shard_map/psum | solution.py:449
  3672.8 45.2 %copy-start.54 = (bf16[768,384]{1,0:T(8,128)(2,1)S(1)}, bf16[768,384]{1,0:T(8,128)(2,1)}, u32[]{:S(2)}) copy-start(bf16[768,384]{1,0:T(8,128)(2,1)} %all_gather.92) | copy-start | bytes 1769476
  3718.0 89.7 %reduce-scatter.65.cloned.1.call-start = ((), (), s32[]{:S(2)}) async-start(), calls=%async_computation.60 | async-start | bytes 4718592 | tf_op jit(solution)/shard_map/reduce_scatter | solution.py:85
  3724.3 98.2 %reduce-scatter.59.cloned.1.call-start = ((), (), s32[]{:S(2)}) async-start(), calls=%async_computation.54 | async-start | bytes 4718592 | tf_op jit(solution)/shard_map/reduce_scatter | solution.py:85
  3804.5 18.0 copy-start.20
  3804.5 18.0 copy-start.162
  3807.7 45.4 %copy-start.50 = (f32[1,1024,384]{2,1,0:T(8,128)S(1)}, f32[1,1024,384]{2,1,0:T(8,128)}, u32[]{:S(2)}) copy-start(f32[1,1024,384]{2,1,0:T(8,128)} %reduce-scatter.65.cloned.1.call-done) | copy-start | bytes 4718596
  (222 other events, 775.3 us)
Sparse Core Ops, SparseCore 0:
  14.5 12.3 all-gather.27
  29.0 10.9 all-gather.15
  1004.4 12.3 reduce-scatter.48
  1051.5 12.3 reduce-scatter.42
  1073.0 10.9 all-gather.17
  1146.6 9.8 all-gather.29
  1168.0 10.9 reduce-scatter.44
  1197.9 11.5 reduce-scatter.50
  1451.3 11.0 all-gather.35
  1464.3 11.0 all-gather.41
  1492.9 13.0 reduce-scatter.56
  1522.3 13.0 reduce-scatter.62
  3718.1 76.5 all-reduce.20
  3796.7 10.8 reduce-scatter.64
  3810.4 12.0 reduce-scatter.58
Sparse Core Ops, SparseCore 1:
  1199.8 37.5 all-gather.21
  1239.4 8.5 all-gather.19
  1249.4 38.1 all-gather.23
  1289.1 35.8 all-gather.25
  1327.1 8.5 all-gather.31
  1338.5 11.9 reduce-scatter.46
  1352.6 12.0 reduce-scatter.52
  1385.8 10.9 all-gather.39
  1398.7 10.8 all-gather.33
  1411.9 11.9 reduce-scatter.60
  1426.9 11.9 reduce-scatter.54
  1546.1 10.8 all-gather.37
  1559.0 10.8 all-gather.43
  1572.1 36.5 reduce-scatter.98
  1611.0 34.1 reduce-scatter.100
  1647.5 34.1 reduce-scatter.96
  1684.0 34.1 reduce-scatter.94
  1720.6 34.1 reduce-scatter.92
  1756.9 34.1 reduce-scatter.90
  1793.5 20.9 reduce-scatter.108
  1816.6 20.3 reduce-scatter.104
  1839.1 20.3 reduce-scatter.102
  1861.7 20.3 reduce-scatter.106
  1884.3 20.3 reduce-scatter.84
  1906.9 20.3 reduce-scatter.82
  1929.5 20.3 reduce-scatter.88
  1952.2 20.3 reduce-scatter.86
  1974.7 20.3 reduce-scatter.78
  1997.2 20.3 reduce-scatter.80
  2596.6 23.2 reduce-scatter.66
  3602.7 23.2 reduce-scatter.68
  3628.1 20.3 reduce-scatter.70
  3650.8 20.3 reduce-scatter.72
  3673.3 20.3 reduce-scatter.74
  3695.9 20.3 reduce-scatter.76
where the time goes:
time: 3940 us; the launch traced here: 3870 us
  local copies, waits for them, and re-layouts  2680 us (68%)
  matrix products  319 us (8%)
  waiting for transfers between devices  308 us (8%)
  other arithmetic  246 us (6%)
  blocking collectives  213 us (5%)
  loops' own time  72.8 us (2%)
    unnamed x456, local copies, waits for them, and re-layouts  2350 us
    while x148, local copies, waits for them, and re-layouts  142 us
    dot_general x16, matrix products, per_block(): jnp.einsum('qhd,khd->hqk', query_block, seq_keys, preferred_element_type=...  91.7 us
  transfers between devices with their start and end apart: 50, of which 20 were waited for; matrix products, arithmetic and copies ran while one was open for 81% of the time, Pallas kernels for 0%

commit v1 on v0

v1 whole, which is shorter than its diff:
```python
import math

import jax
import jax.numpy as jnp
from jax import lax
from jax.experimental import pallas as pl
from jax.experimental.pallas import tpu as pltpu
from jax.sharding import PartitionSpec as P

D = 768
HALF = 384
L = 1024
LE = 256
BUCKETS = 32
SPAN = 1536
EPSILON = 1e-06
MASKED = -1e30
ROOT_TWO_PI = math.sqrt(2.0 / math.pi)
MESH = pl.DeviceIdType.MESH
ROWS = 4
QUAD = 4
BLOCK = D // ROWS
PIECE = BLOCK // QUAD
f32 = jnp.float32
bf16 = jnp.bfloat16
NT = (((1,), (1,)), ((), ()))
NN = (((1,), (0,)), ((), ()))
TN = (((0,), (0,)), ((), ()))
VMEM_LIMIT = 60 * 2**20


def dot(a, b, dims):
    return lax.dot_general(a, b, dims, preferred_element_type=f32)


def lanes(offset, rows=L):
    return pl.BlockSpec((rows, 128), lambda h: (0, offset + h))


def qkv_lanes(which):
    return pl.BlockSpec((L, 128), lambda h: (0, (h // 3) * 9 + 3 * which + h % 3))


def kv_lanes(which):
    return pl.BlockSpec((LE, 128), lambda h: (0, (h // 3) * 6 + 3 * which + h % 3))


def head_of(x, h):
    lane = lax.broadcasted_iota(jnp.int32, x.shape, 1)
    return jnp.where((lane >= 64 * h) & (lane < 64 * h + 64), x, jnp.zeros_like(x))


def transposed(x):
    return x.astype(f32).T.astype(bf16)


def spread_bias(t8_ref, table):
    for h in range(2):
        t = t8_ref[h]
        for m in range(16):
            table[h, 8 * m : 8 * m + 8, :] = pltpu.roll(t, 8 * m, 1)


def allowed_rows(piece_ref, base, rows, width):
    s0 = piece_ref[0]
    s1 = piece_ref[1]
    e0 = piece_ref[2]
    e1 = piece_ref[3]
    c = lax.broadcasted_iota(jnp.int32, (1, width), 1) + base
    last = jnp.where(
        (c >= s0) & (c < e0), e0 - 1, jnp.where((c >= s1) & (c < e1), e1 - 1, 0)
    )
    last = jnp.maximum(c, last)
    return lax.broadcasted_iota(jnp.int32, (rows, width), 0) + base <= last


def extent(qb, width):
    return 512 * ((qb * width) // 512 + 1)


def biased_scores(k_ref, q_head, table, h, base, width, ext, ok):
    s = dot(k_ref[:ext, :], q_head, NT)
    bias = jnp.concatenate(
        [table[h, :, pl.ds(base - 128 * g + 512, width)] for g in range(ext // 128)], axis=0
    )
    s = s + bias
    tail = jnp.where(ok, s[base:], MASKED)
    return tail if base == 0 else jnp.concatenate([s[:base], tail], axis=0)


def softmax_cols(s):
    m = jnp.max(s, axis=0, keepdims=True)
    p = jnp.exp(s - m)
    total = jnp.sum(p, axis=0, keepdims=True)
    return (p.astype(bf16), total, m)


def tasks_of(width, group):
    tasks = [(qb, h) for qb in range(L // width) for h in range(2)]
    return [tasks[i : i + group] for i in range(0, len(tasks), group)]


def self_forward_body(piece_ref, q_ref, k_ref, v_ref, t8_ref, o_ref, lse_ref, table):
    width = 256
    vt = transposed(v_ref[...])
    spread_bias(t8_ref, table)
    oks = [
        allowed_rows(piece_ref, qb * width, extent(qb, width) - qb * width, width)
        for qb in range(L // width)
    ]
    outs = {}
    for group in tasks_of(width, 8):
        scored = [
            biased_scores(
                k_ref,
                head_of(q_ref[pl.ds(qb * width, width), :], h),
                table,
                h,
                qb * width,
                width,
                extent(qb, width),
                oks[qb],
            )
            for qb, h in group
        ]
        weights = [softmax_cols(s) for s in scored]
        for (qb, h), (p, total, m) in zip(group, weights):
            mixed = dot(vt[64 * h : 64 * h + 64, : extent(qb, width)], p, NN)
            outs[(qb, h)] = mixed * (1.0 / total)
            lse_ref[0, h : h + 1, pl.ds(qb * width, width)] = m + jnp.log(total)
            if h == 1:
                o_ref[pl.ds(qb * width, width), :] = (
                    jnp.concatenate([outs[(qb, 0)], outs[(qb, 1)]], axis=0).T.astype(bf16)
                )


def self_forward(qkv, t8, piece):
    return pl.pallas_call(
        self_forward_body,
        grid=(6,),
        in_specs=[
            pl.BlockSpec(memory_space=pltpu.SMEM),
            qkv_lanes(0),
            qkv_lanes(1),
            qkv_lanes(2),
            pl.BlockSpec((2, 8, SPAN), lambda h: (h, 0, 0)),
        ],
        out_specs=[lanes(0), pl.BlockSpec((1, 2, L), lambda h: (h, 0, 0))],
        out_shape=[
            jax.ShapeDtypeStruct((L, D), bf16),
            jax.ShapeDtypeStruct((6, 2, L), f32),
        ],
        scratch_shapes=[pltpu.VMEM((2, 128, SPAN), f32)],
        compiler_params=pltpu.CompilerParams(vmem_limit_bytes=VMEM_LIMIT),
        name="self_forward",
    )(piece, qkv, qkv, qkv, t8)


def head_deltas(a_ref, da_ref):
    prod = (a_ref[...].astype(f32) * da_ref[...].astype(f32)).T
    return [jnp.sum(prod[64 * h : 64 * h + 64], axis=0, keepdims=True) for h in range(2)]


def self_backward_body(
    piece_ref,
    q_ref,
    k_ref,
    v_ref,
    t8_ref,
    a_ref,
    da_ref,
    lse_ref,
    dq_ref,
    dk_ref,
    dv_ref,
    diag_ref,
    table,
    spans,
    dk_sum,
    dv_sum,
):
    width = 256
    delta = head_deltas(a_ref, da_ref)
    kt = transposed(k_ref[...])
    spread_bias(t8_ref, table)
    spans[...] = jnp.zeros_like(spans)
    dk_sum[...] = jnp.zeros_like(dk_sum)
    dv_sum[...] = jnp.zeros_like(dv_sum)
    for group in tasks_of(width, 2):
        qb = group[0][0]
        base = qb * width
        ext = extent(qb, width)
        ok = allowed_rows(piece_ref, base, ext - base, width)
        q = q_ref[pl.ds(base, width), :]
        da = da_ref[pl.ds(base, width), :]
        scored = [
            biased_scores(k_ref, head_of(q, h), table, h, base, width, ext, ok) for _, h in group
        ]
        dprobs = [dot(v_ref[:ext, :], head_of(da, h), NT) for _, h in group]
        low = []
        for h in range(2):
            p = jnp.exp(scored[h] - lse_ref[0, h : h + 1, pl.ds(base, width)])
            ds = p * (dprobs[h] - delta[h][:, base : base + width])
            for g in range(ext // 128):
                spans[h, :, pl.ds(base - 128 * g + 512, width)] += ds[128 * g : 128 * g + 128]
            low.append((p.astype(bf16), ds.astype(bf16)))
        dks = [dot(ds, q, NN) for _, ds in low]
        dvs = [dot(p, da, NN) for p, _ in low]
        dqs = [dot(kt[64 * h : 64 * h + 64, :ext], low[h][1], NN) for h in range(2)]
        lane = lax.broadcasted_iota(jnp.int32, (ext, 128), 1)
        dk_sum[:ext] += jnp.where(lane < 64, dks[0], dks[1])
        dv_sum[:ext] += jnp.where(lane < 64, dvs[0], dvs[1])
        dq_ref[pl.ds(base, width), :] = jnp.concatenate(dqs, axis=0).T.astype(bf16)
    dk_ref[...] = dk_sum[...].astype(bf16)
    dv_ref[...] = dv_sum[...].astype(bf16)
    for h in range(2):
        total = spans[h, 0:8, :]
        for m in range(1, 16):
            total = total + pltpu.roll(spans[h, 8 * m : 8 * m + 8, :], SPAN - 8 * m, 1)
        diag_ref[h] = total


def self_backward(qkv, t8, piece, mixed, dmixed, lse):
    return pl.pallas_call(
        self_backward_body,
        grid=(6,),
        in_specs=[
            pl.BlockSpec(memory_space=pltpu.SMEM),
            qkv_lanes(0),
            qkv_lanes(1),
            qkv_lanes(2),
            pl.BlockSpec((2, 8, SPAN), lambda h: (h, 0, 0)),
            lanes(0),
            lanes(0),
            pl.BlockSpec((1, 2, L), lambda h: (h, 0, 0)),
        ],
        out_specs=[
            lanes(0),
            lanes(0),
            lanes(0),
            pl.BlockSpec((2, 8, SPAN), lambda h: (h, 0, 0)),
        ],
        out_shape=[jax.ShapeDtypeStruct((L, D), bf16)] * 3
        + [jax.ShapeDtypeStruct((12, 8, SPAN), f32)],
        scratch_shapes=[
            pltpu.VMEM((2, 128, SPAN), f32),
            pltpu.VMEM((2, 128, SPAN), f32),
            pltpu.VMEM((L, 128), f32),
            pltpu.VMEM((L, 128), f32),
        ],
        compiler_params=pltpu.CompilerParams(vmem_limit_bytes=VMEM_LIMIT),
        name="self_backward",
    )(piece, qkv, qkv, qkv, t8, mixed, dmixed, lse)


def cross_forward_body(q_ref, k_ref, v_ref, o_ref, lse_ref):
    width = 256
    vt = transposed(v_ref[...])
    outs = {}
    for group in tasks_of(width, 8):
        scored = [
            dot(k_ref[...], head_of(q_ref[pl.ds(qb * width, width), :], h), NT) for qb, h in group
        ]
        weights = [softmax_cols(s) for s in scored]
        for (qb, h), (p, total, m) in zip(group, weights):
            outs[(qb, h)] = dot(vt[64 * h : 64 * h + 64, :], p, NN) * (1.0 / total)
            lse_ref[0, h : h + 1, pl.ds(qb * width, width)] = m + jnp.log(total)
            if h == 1:
                o_ref[pl.ds(qb * width, width), :] = (
                    jnp.concatenate([outs[(qb, 0)], outs[(qb, 1)]], axis=0).T.astype(bf16)
                )


def cross_forward(queries, key_values):
    return pl.pallas_call(
        cross_forward_body,
        grid=(6,),
        in_specs=[lanes(0), kv_lanes(0), kv_lanes(1)],
        out_specs=[lanes(0), pl.BlockSpec((1, 2, L), lambda h: (h, 0, 0))],
        out_shape=[
            jax.ShapeDtypeStruct((L, D), bf16),
            jax.ShapeDtypeStruct((6, 2, L), f32),
        ],
        compiler_params=pltpu.CompilerParams(vmem_limit_bytes=VMEM_LIMIT),
        name="cross_forward",
    )(queries, key_values, key_values)


def cross_backward_body(q_ref, k_ref, v_ref, a_ref, da_ref, lse_ref, dq_ref, dk_ref, dv_ref):
    width = 256
    delta = head_deltas(a_ref, da_ref)
    kt = transposed(k_ref[...])
    lane = lax.broadcasted_iota(jnp.int32, (LE, 128), 1)
    outs = {}
    dks = [None, None]
    dvs = [None, None]
    for group in tasks_of(width, 4):
        scored = [
            dot(k_ref[...], head_of(q_ref[pl.ds(qb * width, width), :], h), NT) for qb, h in group
        ]
        dprobs = [
            dot(v_ref[...], head_of(da_ref[pl.ds(qb * width, width), :], h), NT) for qb, h in group
        ]
        low = []
        for (qb, h), s, dp in zip(group, scored, dprobs):
            p = jnp.exp(s - lse_ref[0, h : h + 1, pl.ds(qb * width, width)])
            ds = p * (dp - delta[h][:, qb * width : (qb + 1) * width])
            low.append((p.astype(bf16), ds.astype(bf16)))
        for (qb, h), (p, ds) in zip(group, low):
            dk = dot(ds, q_ref[pl.ds(qb * width, width), :], NN)
            dv = dot(p, da_ref[pl.ds(qb * width, width), :], NN)
            dks[h] = dk if dks[h] is None else dks[h] + dk
            dvs[h] = dv if dvs[h] is None else dvs[h] + dv
            outs[(qb, h)] = dot(kt[64 * h : 64 * h + 64, :], ds, NN)
            if h == 1:
                dq_ref[pl.ds(qb * width, width), :] = (
                    jnp.concatenate([outs[(qb, 0)], outs[(qb, 1)]], axis=0).T.astype(bf16)
                )
    dk_ref[...] = jnp.where(lane < 64, dks[0], dks[1]).astype(bf16)
    dv_ref[...] = jnp.where(lane < 64, dvs[0], dvs[1]).astype(bf16)


def cross_backward(queries, key_values, mixed, dmixed, lse):
    return pl.pallas_call(
        cross_backward_body,
        grid=(6,),
        in_specs=[
            lanes(0),
            kv_lanes(0),
            kv_lanes(1),
            lanes(0),
            lanes(0),
            pl.BlockSpec((1, 2, L), lambda h: (h, 0, 0)),
        ],
        out_specs=[lanes(0), lanes(0, LE), lanes(0, LE)],
        out_shape=[jax.ShapeDtypeStruct((L, D), bf16)] + [jax.ShapeDtypeStruct((LE, D), bf16)] * 2,
        compiler_params=pltpu.CompilerParams(vmem_limit_bytes=VMEM_LIMIT),
        name="cross_backward",
    )(queries, key_values, key_values, mixed, dmixed, lse)


def place():
    dp = lax.axis_index("dp")
    return (dp, dp % QUAD, lax.axis_index("row"), lax.axis_index("col"))


def quad_mate(dp, quarter, flip):
    return dp - quarter + (quarter ^ flip)


def greet_all(dp, quarter, row, col):
    barrier = pltpu.get_barrier_semaphore()
    for s in range(1, ROWS):
        pl.semaphore_signal(
            barrier, inc=1, device_id=(dp, (row + s) % ROWS, col), device_id_type=MESH
        )
    for k in range(1, QUAD):
        pl.semaphore_signal(
            barrier, inc=1, device_id=(quad_mate(dp, quarter, k), row, col), device_id_type=MESH
        )
    pl.semaphore_signal(barrier, inc=1, device_id=(dp, row, 1 - col), device_id_type=MESH)
    pl.semaphore_wait(barrier, ROWS + QUAD - 1)


def gather_body(count, *refs):
    blocks = refs[:count]
    wholes = refs[count : 2 * count]
    z_send, z_recv, q_send, q_recv, c_send, c_recv, local_sem = refs[2 * count :]
    dp, quarter, row, col = place()
    greet_all(dp, quarter, row, col)
    partner = (dp, row, 1 - col)
    started = []

    def begin(copy):
        copy.start()
        started.append(copy)
        return copy

    def part(i, r, q):
        wide = blocks[i].shape[1]
        at = pl.multiple_of(r * BLOCK + q * PIECE, PIECE)
        return wholes[i].at[pl.ds(at, PIECE), pl.ds(pl.multiple_of(col * wide, 128), wide)]

    z_copies = {}
    own = []
    c_copies = []
    for i in range(count):
        wide = blocks[i].shape[1]
        whole_block = wholes[i].at[
            pl.ds(pl.multiple_of(row * BLOCK, BLOCK), BLOCK),
            pl.ds(pl.multiple_of(col * wide, 128), wide),
        ]
        for s in range(1, ROWS):
            z_copies[(i, s)] = begin(
                pltpu.make_async_remote_copy(
                    src_ref=blocks[i].at[pl.ds(pl.multiple_of(quarter * PIECE, PIECE), PIECE), :],
                    dst_ref=part(i, row, quarter),
                    send_sem=z_send.at[i, s - 1],
                    recv_sem=z_recv.at[i, s - 1],
                    device_id=(dp, (row + s) % ROWS, col),
                    device_id_type=MESH,
                )
            )
        c_copies.append(
            begin(
                pltpu.make_async_remote_copy(
                    src_ref=blocks[i],
                    dst_ref=whole_block,
                    send_sem=c_send.at[i, 0, 0],
                    recv_sem=c_recv.at[i, 0, 0],
                    device_id=partner,
                    device_id_type=MESH,
                )
            )
        )
        local = pltpu.make_async_copy(blocks[i], whole_block, local_sem.at[i])
        local.start()
        own.append(local)
    q_copies = {}

    def hand_over(i, s, k, r):
        ref = part(i, r, quarter ^ k)
        c_copies.append(
            begin(
                pltpu.make_async_remote_copy(
                    src_ref=ref,
                    dst_ref=ref,
                    send_sem=c_send.at[i, s, k],
                    recv_sem=c_recv.at[i, s, k],
                    device_id=partner,
                    device_id_type=MESH,
                )
            )
        )

    def spread(i):
        for s in range(1, ROWS):
            z_copies[(i, s)].wait_recv()
            r = (row - s + ROWS) % ROWS
            ref = part(i, r, quarter)
            for k in range(1, QUAD):
                q_copies[(i, s, k)] = begin(
                    pltpu.make_async_remote_copy(
                        src_ref=ref,
                        dst_ref=ref,
                        send_sem=q_send.at[i, s - 1, k - 1],
                        recv_sem=q_recv.at[i, s - 1, k - 1],
                        device_id=(quad_mate(dp, quarter, k), row, col),
                        device_id_type=MESH,
                    )
                )
            hand_over(i, s, 0, r)

    def share(i):
        for s in range(1, ROWS):
            for k in range(1, QUAD):
                q_copies[(i, s, k)].wait_recv()
                hand_over(i, s, k, (row - s + ROWS) % ROWS)

    for i in range(count):
        spread(i)
        if i > 0:
            share(i - 1)
    share(count - 1)
    for copy in own:
        copy.wait()
    for copy in c_copies:
        copy.wait_recv()
    for copy in started:
        copy.wait_send()


def gather_weights(blocks, number):
    count = len(blocks)
    wholes = [jax.ShapeDtypeStruct((D, 2 * b.shape[1]), b.dtype) for b in blocks]
    dma = pltpu.SemaphoreType.DMA
    return pl.pallas_call(
        lambda *refs: gather_body(count, *refs),
        out_shape=wholes,
        in_specs=[pl.BlockSpec(memory_space=pl.ANY)] * count,
        out_specs=[pl.BlockSpec(memory_space=pl.ANY)] * count,
        scratch_shapes=[
            dma((count, ROWS - 1)),
            dma((count, ROWS - 1)),
            dma((count, ROWS - 1, QUAD - 1)),
            dma((count, ROWS - 1, QUAD - 1)),
            dma((count, ROWS, QUAD)),
            dma((count, ROWS, QUAD)),
            dma((count,)),
        ],
        compiler_params=pltpu.CompilerParams(collective_id=number, has_side_effects=True),
        name="gather_weights",
    )(*blocks)


def swap_features(x, col):
    own = lax.dynamic_index_in_dim(x, col, 0, keepdims=False)
    other = lax.dynamic_index_in_dim(x, 1 - col, 0, keepdims=False)
    came = lax.ppermute(other, "col", [(0, 1), (1, 0)])
    return jnp.where(
        col == 0, jnp.concatenate([own, came], axis=1), jnp.concatenate([came, own], axis=1)
    )


def swap_back(y, col):
    own = lax.dynamic_slice_in_dim(y, col * HALF, HALF, 1)
    other = lax.dynamic_slice_in_dim(y, (1 - col) * HALF, HALF, 1)
    came = lax.ppermute(other, "col", [(0, 1), (1, 0)])
    return jnp.where(col == 0, jnp.stack([own, came]), jnp.stack([came, own]))


def inverse_rms(v):
    return lax.rsqrt(jnp.mean(v * v, axis=-1, keepdims=True) + EPSILON)


def norm_backward(v, r, gain, dn):
    inner = jnp.sum(dn * gain * v, axis=-1, keepdims=True)
    dv = dn * gain * r - v * (r * r * r) * (inner / D)
    return (dv, jnp.sum(dn * v * r, axis=0))


def gelu_parts(t):
    inner = ROOT_TWO_PI * (t + 0.044715 * t * t * t)
    th = jnp.tanh(inner)
    value = 0.5 * t * (1.0 + th)
    slope = 0.5 * (1.0 + th) + 0.5 * t * (1.0 - th * th) * ROOT_TWO_PI * (
        1.0 + 3.0 * 0.044715 * t * t
    )
    return (value, slope)


def body(
    hidden_in,
    encoded,
    cotangent,
    piece_start,
    image_piece_lengths,
    bucket_table,
    self_query,
    self_key,
    self_value,
    self_out,
    rel_weight,
    cross_query,
    cross_key,
    cross_value,
    cross_out,
    ffn_gate,
    ffn_up,
    ffn_down,
    gain_self,
    gain_cross,
    gain_ffn,
    gain_final,
):
    col = lax.axis_index("col")
    row = lax.axis_index("row")
    blocks = (
        jnp.concatenate([self_query, self_key, self_value], axis=1),
        self_out.T,
        cross_query,
        jnp.concatenate([cross_key, cross_value], axis=1),
        cross_out.T,
        jnp.concatenate([ffn_gate, ffn_up], axis=1),
        ffn_down.T,
    )
    w_qkv, w_out_t, c_query, c_kv, c_out_t, f_gu, f_down_t = gather_weights(blocks, 0)
    small = lax.all_gather(
        jnp.concatenate([gain_self, gain_cross, gain_ffn, gain_final]), "col", axis=0
    )
    gains = small.reshape(2, 4, HALF).transpose(1, 0, 2).reshape(4, D)
    g_self, g_cross, g_ffn, g_final = gains[0], gains[1], gains[2], gains[3]
    w_rel = lax.all_gather(
        lax.all_gather(rel_weight, "row", axis=0, tiled=True), "col", axis=1, tiled=True
    )
    onehot = (
        bucket_table[:SPAN, None] == jnp.arange(BUCKETS, dtype=jnp.int32)[None, :]
    ).astype(f32)
    bias_of = jnp.dot(onehot, w_rel.astype(f32), precision=lax.Precision.HIGHEST).T
    flipped = bias_of[:, ::-1]
    t8 = jnp.stack([jnp.roll(flipped, s, axis=1) for s in range(8)], axis=1)
    starts = lax.dynamic_index_in_dim(piece_start, col, 0, keepdims=False)
    lengths = lax.dynamic_index_in_dim(image_piece_lengths, col, 0, keepdims=False)
    piece = jnp.concatenate([starts, starts + lengths])

    x = swap_features(hidden_in, col).astype(f32)
    enc = swap_features(encoded, col)
    grad_out = swap_features(cotangent, col).astype(f32)

    r1 = inverse_rms(x)
    n1 = (x * r1 * g_self).astype(bf16)
    qkv = dot(n1, w_qkv, NN).astype(bf16)
    a1, lse1 = self_forward(qkv, t8, piece)
    h1 = x + dot(a1, w_out_t, NT)
    r2 = inverse_rms(h1)
    n2 = (h1 * r2 * g_cross).astype(bf16)
    q2 = dot(n2, c_query, NN).astype(bf16)
    kv2 = dot(enc, c_kv, NN).astype(bf16)
    a2, lse2 = cross_forward(q2, kv2)
    h2 = h1 + dot(a2, c_out_t, NT)
    r3 = inverse_rms(h2)
    n3 = (h2 * r3 * g_ffn).astype(bf16)
    gu = dot(n3, f_gu, NN).reshape(L, 2, 2, 1024)
    gate, up = gu[:, :, 0], gu[:, :, 1]
    act, slope = gelu_parts(gate)
    mid = (act * up).astype(bf16).reshape(L, 2048)
    h3 = h2 + dot(mid, f_down_t, NT)
    r4 = inverse_rms(h3)
    output = (h3 * r4 * g_final).astype(bf16)

    dh3, dg_final = norm_backward(h3, r4, g_final, grad_out)
    e3 = dh3.astype(bf16)
    gr_down = dot(e3, mid, TN)
    dmid = dot(e3, f_down_t, NN).astype(bf16).astype(f32).reshape(L, 2, 1024)
    dgu = jnp.stack([dmid * up * slope, dmid * act], axis=2).astype(bf16).reshape(L, 4096)
    gr_gu = dot(n3, dgu, TN)
    dn3 = dot(dgu, f_gu, NT)
    back3, dg_ffn = norm_backward(h2, r3, g_ffn, dn3)
    dh2 = dh3 + back3
    e2 = dh2.astype(bf16)
    gr_co = dot(e2, a2, TN)
    da2 = dot(e2, c_out_t, NN).astype(bf16)
    dq2, dk2, dv2 = cross_backward(q2, kv2, a2, da2, lse2)
    gr_cq = dot(n2, dq2, TN)
    dkv2 = jnp.concatenate([dk2[:, :HALF], dv2[:, :HALF], dk2[:, HALF:], dv2[:, HALF:]], axis=1)
    gr_ckv = dot(enc, dkv2, TN)
    enc_grad = dot(dkv2, c_kv, NT)
    dn2 = dot(dq2, c_query, NT)
    back2, dg_cross = norm_backward(h1, r2, g_cross, dn2)
    dh1 = dh2 + back2
    e1 = dh1.astype(bf16)
    gr_out = dot(e1, a1, TN)
    da1 = dot(e1, w_out_t, NN).astype(bf16)
    dq1, dk1, dv1, diag = self_backward(qkv, t8, piece, a1, da1, lse1)
    dqkv = jnp.concatenate(
        [part[:, HALF * c : HALF * (c + 1)] for c in range(2) for part in (dq1, dk1, dv1)], axis=1
    )
    gr_qkv = dot(n1, dqkv, TN)
    dn1 = dot(dqkv, w_qkv, NT)
    back1, dg_self = norm_backward(x, r1, g_self, dn1)
    hidden_grad = dh1 + back1

    spans = sum(jnp.roll(diag[:, s], -s, axis=1) for s in range(8))[:, ::-1]
    gr_rel = jnp.dot(onehot.T, spans.T, precision=lax.Precision.HIGHEST)

    def reduced(g):
        g = g.astype(bf16)
        g = lax.psum_scatter(g, "col", scatter_dimension=1, tiled=True)
        g = lax.psum_scatter(g, "row", scatter_dimension=0, tiled=True)
        return lax.psum(g, "dp").astype(f32)

    gr_qkv = reduced(gr_qkv)
    gr_out = reduced(gr_out).T
    gr_cq = reduced(gr_cq)
    gr_ckv = reduced(gr_ckv)
    gr_co = reduced(gr_co).T
    gr_gu = reduced(gr_gu)
    gr_down = reduced(gr_down).T
    gain_sums = jnp.stack([dg_self, dg_cross, dg_ffn, dg_final])
    gain_sums, gr_rel = lax.psum((gain_sums, gr_rel), ("dp", "row", "col"))
    gain_sums = lax.dynamic_slice_in_dim(gain_sums, col * HALF, HALF, 1)
    gr_rel = lax.dynamic_slice(gr_rel, (row * 8, col * 6), (8, 6))
    return (
        swap_back(output, col),
        swap_back(hidden_grad, col),
        swap_back(enc_grad, col),
        gr_qkv[:, :HALF],
        gr_qkv[:, HALF : 2 * HALF],
        gr_qkv[:, 2 * HALF :],
        gr_out,
        gr_rel,
        gr_cq,
        gr_ckv[:, :HALF],
        gr_ckv[:, HALF:],
        gr_co,
        gr_gu[:, :1024],
        gr_gu[:, 1024:],
        gr_down,
        gain_sums[0],
        gain_sums[1],
        gain_sums[2],
        gain_sums[3],
    )


def solution(mesh):
    batch = P(("dp", "row"), None, "col")
    inward = P("row", "col")
    outward = P("col", "row")
    gain = P("col")
    weights = (
        (inward,) * 3 + (outward, inward) + (inward,) * 3 + (outward,) + (inward,) * 2 + (outward,)
    )
    placed = (batch,) * 3 + (P(("dp", "row"), None),) * 2 + (P(),) + weights + (gain,) * 4
    return jax.shard_map(
        body,
        mesh=mesh,
        in_specs=placed,
        out_specs=(batch,) * 3 + weights + (gain,) * 4,
        check_vma=False,
    )
```

time: 3940 us -> 825 us (0.21); the launches traced: 3870 us -> 820 us
  local copies, waits for them, and re-layouts: 2680 us -> 141 us
  matrix products: 319 us -> 129 us
  other arithmetic: 246 us -> 67.9 us
  Pallas kernels: 0 us -> 165 us
  blocking collectives: 213 us -> 58 us
  loops' own time: 72.8 us -> 0 us
  waiting for transfers between devices: 308 us -> 241 us
    unnamed x456 -> x189, local copies, waits for them, and re-layouts: 2350 us -> 67.4 us
    dot_general x125 -> x23, matrix products: 319 us -> 129 us  [the longest x21 126 us: dot(): return lax.dot_general(a, b, dims, preferred_element_type=f32)]
    pallas_call x0 -> x5, Pallas kernels: none -> 165 us  [the longest x1 94.4 us: gather_weights(): pl.pallas_call(lambda *refs: gather_body(count, *refs), out_shape=wholes,...]
    while x152 -> x0, local copies, waits for them, and re-layouts: 149 us -> none
    all_gather x10 -> x2, blocking collectives: 138 us -> 3.76 us  [the longest x1 1.98 us: body(): lax.all_gather(jnp.concatenate([gain_self, gain_cross, gain_ffn, gain_fin...]
    all_gather x15 -> x0, waiting for transfers between devices: 112 us -> none  [the longest x1 33.9 us: body(): lax.all_gather(ffn_up, 'row', axis=0, tiled=True)]
    reduce_sum x22 -> x2, other arithmetic: 82.8 us -> 4.99 us  [the longest x1 2.96 us: norm_backward(): return (dv, jnp.sum(dn * v * r, axis=0))]
    reduce_scatter x30 -> x10, waiting for transfers between devices: 150 us -> 226 us  [the longest x7 221 us: reduced(): g = lax.psum_scatter(g, 'row', scatter_dimension=0, tiled=True)]
  transfers between devices with their start and end apart: 50 -> 21, of which waited for: 20 -> 9; matrix products, arithmetic and copies ran while one was open for 81% -> 28% of each run, Pallas kernels for 0% -> 20%
where the time goes in v1:
time: 825 us; the launch traced here: 820 us
  waiting for transfers between devices  241 us (29%)
  Pallas kernels  165 us (20%)
  local copies, waits for them, and re-layouts  141 us (17%)
  matrix products  129 us (16%)
  other arithmetic  67.9 us (8%)
  blocking collectives  58 us (7%)
  between operations  15.6 us (2%)
    reduce_scatter x7, waiting for transfers between devices, reduced(): g = lax.psum_scatter(g, 'row', scatter_dimension=0, tiled=True)  221 us
    dot_general x21, matrix products, dot(): return lax.dot_general(a, b, dims, preferred_element_type=f32)  126 us
    pallas_call x1, Pallas kernels, gather_weights(): pl.pallas_call(lambda *refs: gather_body(count, *refs), out_shape=wholes,...  94.4 us
    unnamed x189, local copies, waits for them, and re-layouts  67.4 us
    psum x1, blocking collectives, body(): gain_sums, gr_rel = lax.psum((gain_sums, gr_rel), ('dp', 'row', 'col'))  41 us
    pallas_call x1, Pallas kernels, self_backward(): pl.pallas_call(self_backward_body, grid=(6,), in_specs=[pl.BlockSpec(memo...  32.5 us
    pallas_call x1, Pallas kernels, self_forward(): pl.pallas_call(self_forward_body, grid=(6,), in_specs=[pl.BlockSpec(memor...  18.2 us
    reshape x2, local copies, waits for them, and re-layouts, body(): dmid = dot(e3, f_down_t, NN).astype(bf16).astype(f32).reshape(L, 2, 1024)  18 us
  transfers between devices with their start and end apart: 21, of which 9 were waited for; matrix products, arithmetic and copies ran while one was open for 28% of the time, Pallas kernels for 20%

profile of v1, /device:TPU:0, one launch (start us, length us, event | category | flops | bytes accessed | tf_op | source)
XLA Modules:
  0.0 819.9 jit_solution(14723550852072114352)
XLA Ops:
  9.5 2.2 constant_dynamic-slice_fusion.3
  14.6 13.2 %all_gather.14 = bf16[32,6]{1,0:T(8,128)(2,1)S(1)} all-gather(bf16[8,6]{1,0:T(8,128)(2,1)S(1)} %copy-done.64), channel_id=1, replica_groups=mesh['dp'=4,'row'=4,'col'=2] {'row'}, dimensions={0}, use_global_device_ids=true | all-gather | bytes 480 | tf_op jit(solution)/shard_map/all_gather | solution.py:574
  51.3 2.1 pad_maximum_fusion.1.refs_5_
  57.6 2.2 pad_maximum_fusion.3.refs_0_
  59.8 94.4 %gather_weights.1 = (bf16[768,2304]{1,0:T(8,128)(2,1)}, bf16[768,768]{1,0:T(8,128)(2,1)}, bf16[768,768]{1,0:T(8,128)(2,1)}, bf16[768,1536]{1,0:T(8,128)(2,1)}, b...) custom-call(bf16[192,1152]{1,0:T(8,128)(2,1)} %pad_maximum_fusion.3.refs_0_, ...), custom_call_target="tpu_custom_call" | custom-call | tf_op jit(solution)/shard_map/gather_weights/pallas_call | solution.py:477
  156.8 3.7 convolution_convert_fusion.5.k_ref.v_ref
  163.1 7.8 convolution_convert_fusion.1.q_ref.k_ref.v_ref
  171.0 18.2 %self_forward.1 = (bf16[1024,768]{1,0:T(8,128)(2,1)}, f32[6,2,1024]{2,1,0:T(2,128)}) custom-call(s32[4]{0:T(128)} %pad_add_fusion.piece_ref, bf16[1024,2304]{1,0:T(8,128)(2,1)} %convolution_convert_fusion.1.q_ref.k_ref.v_ref, bf16[1024,2304]{1,0:T(8,128)(2,1)} %convolution_convert_fusion.1.q_ref.k_ref.v_ref, ...), custom_call_target="tpu_custom_call" | custom-call | tf_op jit(solution)/shard_map/self_forward/pallas_call | solution.py:138
  189.2 3.8 multiply_reduce_fusion.6
  194.6 2.7 convolution_convert_fusion.8.q_ref
  197.4 8.3 %cross_forward.1 = (bf16[1024,768]{1,0:T(8,128)(2,1)}, f32[6,2,1024]{2,1,0:T(2,128)}) custom-call(bf16[1024,768]{1,0:T(8,128)(2,1)} %convolution_convert_fusion.8.q_ref, bf16[256,1536]{1,0:T(8,128)(2,1)} %convolution_convert_fusion.5.k_ref.v_ref, bf16[256,1536]{1,0:T(8,128)(2,1)} %convolution_convert_fusion.5.k_ref.v_ref), custom_call_target="tpu_custom_call" | custom-call | tf_op jit(solution)/shard_map/cross_forward/pallas_call | solution.py:275
  205.7 5.8 multiply_reduce_fusion.5
  211.5 10.3 %fusion.56 = f32[1024,4096]{0,1:T(8,128)S(1)} fusion(bf16[768,4096]{1,0:T(8,128)(2,1)} %get-tuple-element.44, f32[1024,768]{0,1:T(8,128)} %get-tuple-element.242, f32[768]{0:T(1024)S(1)} %mul.456, f32[1024]{0:T(1024)S(1)} %get-tuple-element.236), kind=kOutput, calls=%fused_computation.164 | convolution fusion | flops 6444810240 | bytes 26221568 | tf_op jit(solution)/shard_map/dot_general | solution.py:33
  221.8 6.6 fusion.60
  228.4 8.7 %copy.232 = f32[1024,2,1,1024]{3,0,2,1:T(8,128)} copy(f32[1024,2,1,1024]{0,3,2,1:T(8,128)} %get-tuple-element.198) | data formatting | bytes 16777216
  237.2 8.6 %fusion.5 = bf16[1024,2048]{0,1:T(8,128)(2,1)} fusion(f32[1024,2,1,1024]{0,3,2,1:T(8,128)} %get-tuple-element.199, f32[1024,2,1,1024]{0,3,2,1:T(8,128)} %get-tuple-element.198), kind=kLoop, calls=%fused_computation.8 | loop fusion | flops 20971520 | bytes 20971520 | tf_op jit(solution)/shard_map/convert_element_type | solution.py:606
  245.8 9.1 %copy.233 = f32[1024,2,1,1024]{3,0,2,1:T(8,128)} copy(f32[1024,2,1,1024]{0,3,2,1:T(8,128)} %get-tuple-element.199) | data formatting | bytes 16777216
  254.8 7.5 multiply_reduce_fusion.4
  262.4 3.0 fusion.18
  265.7 6.1 convert_convert_fusion
  271.8 9.2 %copy.200 = f32[1024,2048]{0,1:T(8,128)} copy(f32[1024,2048]{1,0:T(8,128)} %convert_convert_fusion) | data formatting | bytes 16777216 | tf_op jit(solution)/shard_map/reshape | solution.py:614
  281.0 8.7 %copy.201 = f32[1024,2,1,1024]{3,0,2,1:T(8,128)} copy(f32[1024,2,1,1024]{0,3,1,2:T(8,128)} %bitcast.138) | data formatting | bytes 16777216 | tf_op jit(solution)/shard_map/reshape | solution.py:614
  289.8 13.3 %fusion.12 = (bf16[1024,2,1,1024]{3,0,2,1:T(8,128)(2,1)S(1)}, bf16[1024,2,1,1024]{3,0,2,1:T(8,128)(2,1)}) fusion(f32[1024,2,1,1024]{3,0,2,1:T(8,128)} %copy.232, f32[1024,2,1,1024]{3,0,2,1:T(8,128)} %copy.201, f32[1024,2,1,1024]{3,0,2,1:T(8,128)} %copy.233), kind=kLoop, calls=%fused_computation.15 | loop fusion | flops 48234496 | bytes 33554432 | tf_op jit(solution)/shard_map/convert.4
  303.1 6.2 pad_maximum_fusion
  309.3 11.4 %copy.203 = bf16[1024,2,2,1024]{0,3,2,1:T(8,128)(2,1)} copy(bf16[1024,2,2,1024]{3,0,2,1:T(8,128)(2,1)} %pad_maximum_fusion) | data formatting | bytes 16777216 | tf_op jit(solution)/shard_map/stack | solution.py:615
  320.8 12.7 %multiply_reduce_fusion = (f32[768]{0:T(1024)}, f32[1024]{0:T(1024)S(1)}, f32[1024,768]{0,1:T(8,128)S(1)}) fusion(f32[1024,768]{0,1:T(8,128)} %get-tuple-element.242, f32[1024]{0:T(1024)S(1)} %get-tuple-element.236, f32[768]{0:T(1024)S(1)} %copy-done.56, bf16[768,4096]{1,0:T(8,128)(2,1)} %get-tuple-element.44, bf16[1024,4096]{0,1:T(8,128)(2,1)} %bitcast.141), kind=kOutput, calls=%fused_computation.49 | convolution fusion | flops 6447167488 | bytes 20985856 | tf_op jit(solution)/shard_map/dot_general | solution.py:33
  333.6 4.9 subtract_add_fusion.1
  340.1 2.4 convolution_convert_fusion.9
  342.5 2.4 copy.229
  344.9 4.9 convolution_convert_fusion.7.da_ref
  349.8 11.4 %cross_backward.1 = (bf16[1024,768]{1,0:T(8,128)(2,1)}, bf16[256,768]{1,0:T(8,128)(2,1)}, bf16[256,768]{1,0:T(8,128)(2,1)}) custom-call(bf16[1024,768]{1,0:T(8,128)(2,1)} %convolution_convert_fusion.8.q_ref, bf16[256,1536]{1,0:T(8,128)(2,1)} %convolution_convert_fusion.5.k_ref.v_ref, bf16[256,1536]{1,0:T(8,128)(2,1)} %convolution_convert_fusion.5.k_ref.v_ref, ...), custom_call_target="tpu_custom_call" | custom-call | tf_op jit(solution)/shard_map/cross_backward/pallas_call | solution.py:324
  361.2 4.8 convolution_convert_fusion.10
  366.0 2.4 copy.227
  368.7 5.2 multiply_reduce_fusion.1
  376.3 2.4 convolution_convert_fusion.11
  378.7 2.4 copy.225
  383.2 3.4 convolution_convert_fusion.4
  386.7 8.9 %convolution_convert_fusion.3 = bf16[768,2048]{1,0:T(8,128)(2,1)} fusion(bf16[1024,2048]{0,1:T(8,128)(2,1)} %fusion.5, f32[1024,768]{0,1:T(8,128)S(1)} %copy-done.1, f32[1024]{0:T(1024)S(1)} %copy-done.61, f32[1024]{0:T(1024)S(1)} %get-tuple-element.237, f32[768]{0:T(1024)S(1)} %mul.470, f32[1024]{0:T(1024)S(1)} %get-tuple-element.238, ...), kind=kOutput, calls=%fused_computation.33 | convolution fusion | flops 3235381248 | bytes 12073985 | tf_op jit(solution)/shard_map/dot_general | solution.py:33
  397.4 3.9 convolution_convert_fusion.6.da_ref
  401.3 32.5 %self_backward.1 = (bf16[1024,768]{1,0:T(8,128)(2,1)}, bf16[1024,768]{1,0:T(8,128)(2,1)}, bf16[1024,768]{1,0:T(8,128)(2,1)}, f32[12,8,1536]{2,1,0:T(8,128)}) custom-call(s32[4]{0:T(128)} %pad_add_fusion.piece_ref, bf16[1024,2304]{1,0:T(8,128)(2,1)} %convolution_convert_fusion.1.q_ref.k_ref.v_ref, ...), custom_call_target="tpu_custom_call" | custom-call | tf_op jit(solution)/shard_map/self_backward/pallas_call | solution.py:224
  437.4 2.1 copy-done.44
  439.5 7.6 convolution_convert_fusion.2
  447.1 5.7 copy.223
  453.6 11.9 %convolution_convert_fusion = bf16[768,4096]{1,0:T(8,128)(2,1)} fusion(bf16[1024,4096]{0,1:T(8,128)(2,1)} %bitcast.142, f32[1024,768]{0,1:T(8,128)} %get-tuple-element.242, f32[768]{0:T(1024)S(1)} %copy-done.57, f32[1024]{0:T(1024)S(1)} %get-tuple-element.236), kind=kOutput, calls=%fused_computation.25 | convolution fusion | flops 6447955968 | bytes 17832960 | tf_op jit(solution)/shard_map/dot_general | solution.py:33
  465.5 2.1 copy.230
  467.8 2.1 copy.228
  470.0 2.1 copy.226
  473.5 3.9 copy.224
  477.5 5.1 reduce-scatter.35.cloned.1.call-done
  492.0 9.8 %fusion.27 = (f32[768]{0:T(1024)}, f32[1024]{0:T(1024)S(1)}, f32[1024,768]{0,1:T(8,128)}) fusion(f32[1024]{0:T(1024)} %copy-done.50, bf16[1024,384]{0,1:T(8,128)(2,1)S(1)} %bitcast.152, bf16[1024,384]{0,1:T(8,128)(2,1)} %collective-permute-done, pred[]{:T(512)S(6)} %eq.8, f32[768]{0:T(1024)} %copy-done.52, bf16[1024,2304]{1,0:T(8,128)(2,1)} %copy-done.44, ...), kind=kOutput, calls=%fused_computation.47 | convolution fusion | flops 3636459776 | bytes 12990465 | tf_op jit(solution)/shard_map/dot_general | solution.py:33
  502.3 6.4 reduce-scatter.33.cloned.1.call-done
  508.7 23.3 %reduce-scatter.27.cloned.1.call-done = bf16[192,384]{1,0:T(8,128)(2,1)} async-done(((bf16[768,384]{1,0:T(8,128)(2,1)}), bf16[192,384]{1,0:T(8,128)(2,1)}) %reduce-scatter.27.cloned.1.call-update) | async-done | bytes 147472 | tf_op jit(solution)/shard_map/reduce_scatter | solution.py:649
  532.1 23.1 %reduce-scatter.25.cloned.1.call-done = bf16[192,384]{1,0:T(8,128)(2,1)} async-done(((bf16[768,384]{1,0:T(8,128)(2,1)}), bf16[192,384]{1,0:T(8,128)(2,1)}) %reduce-scatter.25.cloned.1.call-update) | async-done | bytes 147472 | tf_op jit(solution)/shard_map/reduce_scatter | solution.py:649
  555.1 30.1 %reduce-scatter.31.cloned.1.call-done = bf16[192,768]{1,0:T(8,128)(2,1)} async-done(((bf16[768,768]{1,0:T(8,128)(2,1)}), bf16[192,768]{1,0:T(8,128)(2,1)}) %reduce-scatter.31.cloned.1.call-update) | async-done | bytes 294928 | tf_op jit(solution)/shard_map/reduce_scatter | solution.py:649
  585.2 36.3 %reduce-scatter.41.cloned.1.call-done = bf16[192,1024]{1,0:T(8,128)(2,1)} async-done(((bf16[768,1024]{1,0:T(8,128)(2,1)}), bf16[192,1024]{1,0:T(8,128)(2,1)}) %reduce-scatter.41.cloned.1.call-update) | async-done | bytes 393232 | tf_op jit(solution)/shard_map/reduce_scatter | solution.py:649
  621.5 39.8 %reduce-scatter.23.cloned.1.call-done = bf16[192,1152]{1,0:T(8,128)(2,1)} async-done(((bf16[768,1152]{1,0:T(8,128)(2,1)}), bf16[192,1152]{1,0:T(8,128)(2,1)}) %reduce-scatter.23.cloned.1.call-update) | async-done | bytes 442384 | tf_op jit(solution)/shard_map/reduce_scatter | solution.py:649
  661.3 61.5 %reduce-scatter.37.cloned.1.call-done = bf16[192,2048]{1,0:T(8,128)(2,1)} async-done(((bf16[768,2048]{1,0:T(8,128)(2,1)}), bf16[192,2048]{1,0:T(8,128)(2,1)}) %reduce-scatter.37.cloned.1.call-update) | async-done | bytes 786448 | tf_op jit(solution)/shard_map/reduce_scatter | solution.py:649
  722.9 3.8 fusion.24
  726.8 2.1 dynamic-slice_bitcast_fusion
  736.6 41.0 %all-reduce = (f32[32,12]{1,0:T(8,128)S(1)}, f32[4,768]{1,0:T(4,128)S(1)}) all-reduce(f32[32,12]{1,0:T(8,128)S(1)} %fusion.37, f32[4,768]{1,0:T(4,128)S(1)} %pad_maximum_fusion.8), channel_id=1, replica_groups=mesh['dp'=4,'row'=4,'col'=2] {'dp','row','col'}, use_global_device_ids=true, to_apply=%region_14.15 | all-reduce | flops 3456 | bytes 27648 | tf_op jit(solution)/shard_map/psum | solution.py:660
  779.0 2.1 maximum_select_fusion.4
  782.9 3.6 maximum_select_fusion
  786.5 2.4 copy.218
  788.9 14.1 %all-reduce.4.cloned.1.call-done = (bf16[192,1152]{1,0:T(8,128)(2,1)}, bf16[192,768]{1,0:T(8,128)(2,1)}, bf16[192,2048]{1,0:T(8,128)(2,1)}, bf16[384,192]{0,1:T(...) async-done(((bf16[192,1152]{1,0:T(8,128)(2,1)}, bf16[192,768]{1,0:T(8,128)(2,1)}, bf16[192,2048]{1,0:T(8,128)(2,1)}, ...) | async-done | bytes 2359312 | tf_op jit(solution)/shard_map/psum | solution.py:650
  (332 shorter events, 84.4 us)
Async XLA Ops:
  7.2 458.3 %reduce-scatter.49.cloned.1.call-start = ((), (), s32[]{:S(2)}) async-start(), calls=%async_computation.27 | async-start | bytes 1769472
  9.0 147.8 %collective-permute-start.1 = (bf16[256,384]{1,0:T(8,128)(2,1)}, bf16[256,384]{1,0:T(8,128)(2,1)}, u32[]{:S(2)}, u32[]{:S(2)}) collective-permute-start(bf16[256,384]{1,0:T(8,128)(2,1)} %get-tuple-element.228), channel_id=1, source_target_pairs={{0,1},{1,0},{2,3},{3,2},{4,5},{5,4},{6,7},{7,6},{8,9},{9,8},{10,11... | collective-permute-start | bytes 589832 | tf_op jit(solution)/shard_map/ppermute | solution.py:499
  11.7 18.1 %copy-start.76 = (s32[2047]{0:T(1024)S(1)}, s32[2047]{0:T(1024)}, u32[]{:S(2)}) copy-start(s32[2047]{0:T(1024)} %param.27) | copy-start | bytes 24568
  11.7 20.4 %copy-start.65 = (f32[384]{0:T(512)S(1)}, f32[384]{0:T(512)}, u32[]{:S(2)}) copy-start(f32[384]{0:T(512)} %param.43) | copy-start | bytes 4612
  11.7 20.4 %copy-start.66 = (f32[384]{0:T(512)S(1)}, f32[384]{0:T(512)}, u32[]{:S(2)}) copy-start(f32[384]{0:T(512)} %param.42) | copy-start | bytes 4612
  11.7 20.4 %copy-start.67 = (f32[384]{0:T(512)S(1)}, f32[384]{0:T(512)}, u32[]{:S(2)}) copy-start(f32[384]{0:T(512)} %param.41) | copy-start | bytes 4612
  11.7 20.3 %copy-start.68 = (f32[384]{0:T(512)S(1)}, f32[384]{0:T(512)}, u32[]{:S(2)}) copy-start(f32[384]{0:T(512)} %param.40) | copy-start | bytes 4612
  12.9 147.6 %collective-permute-start = (bf16[1024,384]{0,1:T(8,128)(2,1)}, bf16[1024,384]{0,1:T(8,128)(2,1)}, u32[]{:S(2)}, u32[]{:S(2)}) collective-permute-start(bf16[1024,384]{0,1:T(8,128)(2,1)} %bitcast.158), channel_id=1, source_target_pairs={{0,1},{1,0},{2,3},{3,2},{4,5},{5,4},{6,7},{7,6},{8,9},{9,8},{10,11... | collective-permute-start | bytes 2359304 | tf_op jit(solution)/shard_map/ppermute | solution.py:499
  14.1 36.4 %copy-start.42 = (bf16[192,384]{1,0:T(8,128)(2,1)S(1)}, bf16[192,384]{1,0:T(8,128)(2,1)}, u32[]{:S(2)}) copy-start(bf16[192,384]{1,0:T(8,128)(2,1)} %param.35) | copy-start | bytes 442372
  14.1 36.4 %copy-start.43 = (bf16[192,384]{1,0:T(8,128)(2,1)S(1)}, bf16[192,384]{1,0:T(8,128)(2,1)}, u32[]{:S(2)}) copy-start(bf16[192,384]{1,0:T(8,128)(2,1)} %param.34) | copy-start | bytes 442372
  14.1 248.2 %collective-permute-start.3 = (bf16[1024,384]{0,1:T(8,128)(2,1)}, bf16[1024,384]{0,1:T(8,128)(2,1)S(1)}, u32[]{:S(2)}, u32[]{:S(2)}) collective-permute-start(bf16[1024,384]{0,1:T(8,128)(2,1)} %bitcast.157), channel_id=1, source_target_pairs={{0,1},{1,0},{2,3},{3,2},{4,5},{5,4},{6,7},{7,6},{8,9},{9,8},{10,11... | collective-permute-start | bytes 2359304 | tf_op jit(solution)/shard_map/ppermute | solution.py:499
  54.3 157.1 %copy-start.55 = (f32[768]{0:T(1024)}, f32[768]{0:T(1024)S(1)}, u32[]{:S(2)}) copy-start(f32[768]{0:T(1024)S(1)} %mul.456) | copy-start | bytes 9220
  54.4 138.6 %copy-start.58 = (f32[768]{0:T(1024)}, f32[768]{0:T(1024)S(1)}, u32[]{:S(2)}) copy-start(f32[768]{0:T(1024)S(1)} %mul.450) | copy-start | bytes 9220
  54.4 108.7 %copy-start.52 = (f32[768]{0:T(1024)}, f32[768]{0:T(1024)S(1)}, u32[]{:S(2)}) copy-start(f32[768]{0:T(1024)S(1)} %mul.444) | copy-start | bytes 9220
  57.2 208.1 %copy-start.6 = (bf16[1,1024,384]{1,2,0:T(8,128)(2,1)}, bf16[1,1024,384]{1,2,0:T(8,128)(2,1)S(1)}, u32[]{:S(2)}) copy-start(bf16[1,1024,384]{1,2,0:T(8,128)(2,1)S(1)} %copy.198) | copy-start | bytes 2359300
  57.2 99.0 %copy-start.69 = (s32[2,2]{1,0:T(2,128)S(1)}, s32[2,2]{1,0:T(2,128)}, u32[]{:S(2)}) copy-start(s32[2,2]{1,0:T(2,128)} %param.26) | copy-start | bytes 52
  57.3 99.0 %copy-start.70 = (s32[2,2]{1,0:T(2,128)S(1)}, s32[2,2]{1,0:T(2,128)}, u32[]{:S(2)}) copy-start(s32[2,2]{1,0:T(2,128)} %param.25) | copy-start | bytes 52
  57.6 131.6 %copy-start.8 = (bf16[1,1024,384]{1,2,0:T(8,128)(2,1)}, bf16[1,1024,384]{1,2,0:T(8,128)(2,1)S(1)}, u32[]{:S(2)}) copy-start(bf16[1,1024,384]{1,2,0:T(8,128)(2,1)S(1)} %copy.183) | copy-start | bytes 2359300
  57.6 96.7 %copy-start.30 = (f32[12,1,1536]{2,1,0:T(1,128)S(1)}, f32[12,1,1536]{2,1,0:T(1,128)}, u32[]{:S(2)}) copy-start(f32[12,1,1536]{2,1,0:T(1,128)} %copy.188) | copy-start | bytes 221188
  57.6 96.7 %copy-start.31 = (f32[12,1,1536]{2,1,0:T(1,128)S(1)}, f32[12,1,1536]{2,1,0:T(1,128)}, u32[]{:S(2)}) copy-start(f32[12,1,1536]{2,1,0:T(1,128)} %copy.186) | copy-start | bytes 221188
  57.6 96.7 %copy-start.32 = (f32[12,1,1536]{2,1,0:T(1,128)S(1)}, f32[12,1,1536]{2,1,0:T(1,128)}, u32[]{:S(2)}) copy-start(f32[12,1,1536]{2,1,0:T(1,128)} %copy.187) | copy-start | bytes 221188
  57.6 99.2 %copy-start.33 = (bf16[256,384]{1,0:T(8,128)(2,1)S(1)}, bf16[256,384]{1,0:T(8,128)(2,1)}, u32[]{:S(2)}) copy-start(bf16[256,384]{1,0:T(8,128)(2,1)} %get-tuple-element.227) | copy-start | bytes 589828
  156.8 6.3 copy-start.71
  163.1 7.8 copy-start.50
  189.2 5.5 copy-start.75
  262.3 3.3 copy-start.73
  262.4 9.4 %copy-start.12 = (bf16[1024,384]{0,1:T(8,128)(2,1)}, bf16[1024,384]{0,1:T(8,128)(2,1)S(1)}, u32[]{:S(2)}) copy-start(bf16[1024,384]{0,1:T(8,128)(2,1)S(1)} %collective-permute-done.3) | copy-start | bytes 2359300
  265.4 68.2 %copy-start.60 = (f32[1024]{0:T(1024)}, f32[1024]{0:T(1024)S(1)}, u32[]{:S(2)}) copy-start(f32[1024]{0:T(1024)S(1)} %broadcast_multiply_fusion.3) | copy-start | bytes 12292
  309.3 11.4 %copy-start.56 = (f32[768]{0:T(1024)S(1)}, f32[768]{0:T(1024)}, u32[]{:S(2)}) copy-start(f32[768]{0:T(1024)} %copy-done.55) | copy-start | bytes 9220
  320.8 12.8 %copy-start.1 = (f32[1024,768]{0,1:T(8,128)S(1)}, f32[1024,768]{0,1:T(8,128)}, u32[]{:S(2)}) copy-start(f32[1024,768]{0,1:T(8,128)} %copy-done) | copy-start | bytes 9437188
  320.8 12.8 %copy-start.7 = (bf16[1,1024,384]{1,2,0:T(8,128)(2,1)S(1)}, bf16[1,1024,384]{1,2,0:T(8,128)(2,1)}, u32[]{:S(2)}) copy-start(bf16[1,1024,384]{1,2,0:T(8,128)(2,1)} %copy-done.6) | copy-start | bytes 2359300
  320.8 12.8 %copy-start.13 = (bf16[1024,384]{0,1:T(8,128)(2,1)S(1)}, bf16[1024,384]{0,1:T(8,128)(2,1)}, u32[]{:S(2)}) copy-start(bf16[1024,384]{0,1:T(8,128)(2,1)} %copy-done.12) | copy-start | bytes 2359300
  320.8 12.8 %copy-start.15 = (f32[1024,768]{0,1:T(8,128)S(1)}, f32[1024,768]{0,1:T(8,128)}, u32[]{:S(2)}) copy-start(f32[1024,768]{0,1:T(8,128)} %get-tuple-element.242) | copy-start | bytes 9437188
  333.6 6.5 copy-start.23
  344.9 122.9 %reduce-scatter.47.cloned.1.call-start = ((), (), s32[]{:S(2)}) async-start(), calls=%async_computation.26 | async-start | bytes 1769472
  349.8 11.4 %copy-start.59 = (f32[768]{0:T(1024)S(1)}, f32[768]{0:T(1024)}, u32[]{:S(2)}) copy-start(f32[768]{0:T(1024)} %copy-done.58) | copy-start | bytes 9220
  368.5 101.5 %reduce-scatter.45.cloned.1.call-start = ((), (), s32[]{:S(2)}) async-start(), calls=%async_computation.25 | async-start | bytes 1769472
  368.7 5.2 copy-start.5
  368.7 5.2 copy-start.17
  378.7 3.6 copy-start.25
  381.2 91.0 %reduce-scatter.29.cloned.1.call-start = ((), (), s32[]{:S(2)}) async-start(), calls=%async_computation.17 | async-start | bytes 3538944 | tf_op jit(solution)/shard_map/reduce_scatter | solution.py:648
  383.2 3.5 copy-start.61
  386.6 86.3 %reduce-scatter.39.cloned.1.call-start = ((), (), s32[]{:S(2)}) async-start(), calls=%async_computation.22 | async-start | bytes 4718592 | tf_op jit(solution)/shard_map/reduce_scatter | solution.py:648
  395.6 77.9 %reduce-scatter.43.cloned.1.call-start = ((), (), s32[]{:S(2)}) async-start(), calls=%async_computation.24 | async-start | bytes 5308416
  433.8 3.2 copy-start.22
  433.8 3.3 copy-start.21
  452.9 29.7 %reduce-scatter.35.cloned.1.call-start = ((), (), s32[]{:S(2)}) async-start(), calls=%async_computation.20 | async-start | bytes 9437184 | tf_op jit(solution)/shard_map/reduce_scatter | solution.py:648
  465.5 43.3 %reduce-scatter.33.cloned.1.call-start = ((), (), s32[]{:S(2)}) async-start(), calls=%async_computation.19 | async-start | bytes 737280 | tf_op jit(solution)/shard_map/reduce_scatter | solution.py:649
  467.7 64.4 %reduce-scatter.27.cloned.1.call-start = ((), (), s32[]{:S(2)}) async-start(), calls=%async_computation.16 | async-start | bytes 737280 | tf_op jit(solution)/shard_map/reduce_scatter | solution.py:649
  469.9 85.2 %reduce-scatter.25.cloned.1.call-start = ((), (), s32[]{:S(2)}) async-start(), calls=%async_computation.15 | async-start | bytes 737280 | tf_op jit(solution)/shard_map/reduce_scatter | solution.py:649
  472.1 113.1 %reduce-scatter.31.cloned.1.call-start = ((), (), s32[]{:S(2)}) async-start(), calls=%async_computation.18 | async-start | bytes 1474560 | tf_op jit(solution)/shard_map/reduce_scatter | solution.py:649
  472.9 148.6 %reduce-scatter.41.cloned.1.call-start = ((), (), s32[]{:S(2)}) async-start(), calls=%async_computation.23 | async-start | bytes 1966080 | tf_op jit(solution)/shard_map/reduce_scatter | solution.py:649
  473.4 187.9 %reduce-scatter.23.cloned.1.call-start = ((), (), s32[]{:S(2)}) async-start(), calls=%async_computation.14 | async-start | bytes 2211840 | tf_op jit(solution)/shard_map/reduce_scatter | solution.py:649
  477.5 245.4 %reduce-scatter.37.cloned.1.call-start = ((), (), s32[]{:S(2)}) async-start(), calls=%async_computation.21 | async-start | bytes 3932160 | tf_op jit(solution)/shard_map/reduce_scatter | solution.py:649
  482.6 320.4 %all-reduce.4.cloned.1.call-start = ((), (), s32[]{:S(2)}) async-start(), calls=%async_computation.28 | async-start | bytes 4718592 | tf_op jit(solution)/shard_map/psum | solution.py:650
  482.7 9.3 %copy-start.10 = (bf16[1,1024,384]{1,2,0:T(8,128)(2,1)S(1)}, bf16[1,1024,384]{1,2,0:T(8,128)(2,1)}, u32[]{:S(2)}) copy-start(bf16[1,1024,384]{1,2,0:T(8,128)(2,1)} %copy-done.8) | copy-start | bytes 2359300
  482.7 9.3 %copy-start.72 = (bf16[768,2304]{1,0:T(8,128)(2,1)S(1)}, bf16[768,2304]{1,0:T(8,128)(2,1)}, u32[]{:S(2)}) copy-start(bf16[768,2304]{1,0:T(8,128)(2,1)} %get-tuple-element.37) | copy-start | bytes 10616836
  726.8 3.1 copy-start.74
  728.9 54.0 %collective-permute-start.4 = (f32[1024,384]{0,1:T(8,128)}, f32[1024,384]{0,1:T(8,128)}, u32[]{:S(2)}, u32[]{:S(2)}) collective-permute-start(f32[1024,384]{0,1:T(8,128)} %get-tuple-element.203), channel_id=1, source_target_pairs={{0,1},{1,0},{2,3},{3,2},{4,5},{5,4},{6,7},{7,6},{8,9},{9,8},{10,11... | collective-permute-start | bytes 4718600 | tf_op jit(solution)/shard_map/ppermute | solution.py:508
  731.6 47.3 %collective-permute-start.5 = (f32[256,384]{1,0:T(8,128)}, f32[256,384]{1,0:T(8,128)}, u32[]{:S(2)}, u32[]{:S(2)}) collective-permute-start(f32[256,384]{1,0:T(8,128)} %get-tuple-element.219), channel_id=1, source_target_pairs={{0,1},{1,0},{2,3},{3,2},{4,5},{5,4},{6,7},{7,6},{8,9},{9,8},{10,11... | collective-permute-start | bytes 1179656 | tf_op jit(solution)/shard_map/ppermute | solution.py:508
  731.8 49.3 %collective-permute-start.2 = (bf16[1024,384]{0,1:T(8,128)(2,1)S(1)}, bf16[1024,384]{0,1:T(8,128)(2,1)S(1)}, u32[]{:S(2)}, u32[]{:S(2)}) collective-permute-start(bf16[1024,384]{0,1:T(8,128)(2,1)S(1)} %get-tuple-element.207), channel_id=1, source_target_pairs={{0,1},{1,0},{2,3},{3,2},{4,5},{5,4},{6,7},{7,6},{8,9},{9,8},{10,11... | collective-permute-start | bytes 2359304 | tf_op jit(solution)/shard_map/ppermute | solution.py:508
  803.0 7.0 copy-start.24
  803.0 7.9 copy-start.29
  803.0 8.8 %copy-start.14 = (bf16[192,2048]{1,0:T(8,128)(2,1)S(1)}, bf16[192,2048]{1,0:T(8,128)(2,1)}, u32[]{:S(2)}) copy-start(bf16[192,2048]{1,0:T(8,128)(2,1)} %get-tuple-element.189) | copy-start | bytes 2359300
  (34 other events, 65.4 us)
Sparse Core Ops, SparseCore 0:
  345.0 8.8 reduce-scatter.48
  368.6 8.8 reduce-scatter.46
  381.3 8.8 reduce-scatter.44
  392.4 11.0 reduce-scatter.28
  405.6 12.0 reduce-scatter.38
  453.0 11.4 reduce-scatter.42
  466.9 15.6 reduce-scatter.34
  485.5 23.1 reduce-scatter.32
  511.7 20.3 reduce-scatter.26
  534.9 20.2 reduce-scatter.24
  557.5 27.6 reduce-scatter.30
  587.5 33.9 reduce-scatter.40
  623.9 37.3 reduce-scatter.22
  663.5 59.3 reduce-scatter.36
  726.6 76.3 all-reduce.3
